TPU v7x, 512 devices: a whole 4x4x16 slice. The times are simulated.
512 devices in a mesh: mem: 16 (over y, x), lon: 16 (over z_lo, core), lat: 2 (over z_hi).
Axes of the slice: x: 4, y: 4, z: 16 (z_hi: 2, z_lo: 8; z = z_hi * 8 + z_lo), core: 2. Of those that a mesh axis runs over, the one named last changes fastest.
Arguments:
- prior_sample_set: float32 [128, 8, 8, 2048], P('mem', None, 'lat', 'lon'), may hold values from -18 to 18
- eastward_cfl_number: float32 [8, 8, 2048], P(None, 'lat', 'lon'), may hold values from -0.35 to 0.35
- northward_cfl_number: float32 [8, 8, 2048], P(None, 'lat', 'lon'), may hold values from -0.35 to 0.35
- spreading_number: float32 [8, 8, 2048], P(None, 'lat', 'lon')
- obs_value: float32 [2, 16, 256], P('lat', 'lon'), may hold values from -6 to 6
- obs_site: int32 [2, 16, 256], P('lat', 'lon'), may hold values from 0 to 4095
- neighbours: int32 [8, 2048, 128], P('lat', 'lon'), may hold values from 0 to 2303, as said below
- loc_weight: float32 [8, 2048, 128], P('lat', 'lon'), may hold values from 0.15 to 1
Outputs:
- analysis: float32 [128, 8, 8, 2048], P('mem', None, 'lat', 'lon')
Inputs may be any that keep to these rules, and one draw needn't show every extreme that they name: obs_site[a, b, o] = l * 4 * 128 + i * 128 + j names level l, row i and column j inside block (a, b). `neighbours`: each entry is ((p + 1) * 3 + (t + 1)) * 256 + o with p and t in -1, 0, 1 and o below 256; the block a + p always lies within the grid's latitude blocks.
All inputs are finite; a program needn't handle non-finite values.
Results may differ from a plain program's by a relative error of at most 0.0003.
Values sent between devices are 32-bit elements; how exact they have to be, the bound alone decides.
No kernel may reach another device: no remote copies, remote signals or barrier semaphores. Data moves between devices by JAX's collectives and lax.ppermute only.
A program may use at most 64 MiB of HBM per device.

v0:
```python
import functools

import jax
import jax.numpy as jnp
from jax import lax
from jax.experimental import pallas as pl
from jax.experimental.pallas import tpu as pltpu
from jax.sharding import PartitionSpec as P

STEPS = 4
LANES = 128
OWNED = 32
GROUPS = LANES // OWNED
ROWS = 4
BATCH = 16
MEMBERS_HERE = 8
LEVELS = 8
NOB = 256
PLANE = LEVELS * ROWS
VALUE_ROW = 11 * PLANE
SITE_ROW = VALUE_ROW + 2
EDGE_ROW = SITE_ROW + 6
EDGE_ROWS = 16
PAYLOAD = EDGE_ROW + EDGE_ROWS
COLS = LEVELS * OWNED
SPREAD_ROWS = 136
FAR = -8192
F32 = jnp.float32
BF16 = jnp.bfloat16
VMEM_LIMIT = 40 * 1024 * 1024
PAYLOAD_LIMIT = 60 * 1024 * 1024


def vmem(count):
    return [pl.BlockSpec(memory_space=pltpu.VMEM)] * count


def params():
    return pltpu.CompilerParams(vmem_limit_bytes=VMEM_LIMIT)


def lane_index():
    return lax.broadcasted_iota(jnp.int32, (8, LANES), 1)


def lat_masks():
    here = lax.axis_index("lat")
    return [scalar_mask(here, 0), scalar_mask(here, 1)]


def lon_parity():
    return lax.rem(lax.axis_index("lon"), 2)


def scalar_mask(value, wanted):
    return jnp.full((8, LANES), value, jnp.int32) == wanted


def roll(x, shift):
    shift %= LANES
    return x if shift == 0 else pltpu.roll(x, shift, 1)


def member_rows(own_ref, other_ref, here, level, row):
    start = level * ROWS + row % ROWS
    own = own_ref[pl.ds(start, 8, stride=PLANE), :]
    other = other_ref[pl.ds(start, 8, stride=PLANE), :]
    return jnp.where(here[row // ROWS], own, other)


def coef_rows(own_ref, other_ref, here, which, row):
    start = (MEMBERS_HERE + which) * PLANE + row % ROWS
    own = own_ref[pl.ds(start, 8, stride=ROWS), :]
    other = other_ref[pl.ds(start, 8, stride=ROWS), :]
    return jnp.where(here[row // ROWS], own, other)


def payload_kernel(
    prior_ref,
    east_ref,
    north_ref,
    spread_ref,
    value_ref,
    site_ref,
    ids_ref,
    weight_ref,
    out_ref,
    first_ref,
    second_ref,
    ids_out,
    weight_out,
    value,
    site,
    sems,
):
    owned = pl.ds(pl.multiple_of(lax.axis_index("mem") * OWNED, OWNED), OWNED)
    moves = [
        (prior_ref, out_ref.at[pl.ds(0, MEMBERS_HERE * PLANE), :]),
        *[
            (ref, out_ref.at[pl.ds((MEMBERS_HERE + n) * PLANE, PLANE), :])
            for n, ref in enumerate((east_ref, north_ref, spread_ref))
        ],
        (value_ref, value),
        (site_ref, site),
        (ids_ref.at[owned, :], ids_out),
        (weight_ref.at[owned, :], weight_out),
    ]
    copies = [pltpu.make_async_copy(src, dst, sems.at[n]) for n, (src, dst) in enumerate(moves)]
    for copy in copies:
        copy.start()
    for copy in copies:
        copy.wait()
    values = value[...]
    sites = site[...].astype(F32)
    rest = jnp.zeros((PAYLOAD - SITE_ROW - 2, LANES), F32)
    pieces = [values[:, :LANES], values[:, LANES:], sites[:, :LANES], sites[:, LANES:], rest]
    out_ref[VALUE_ROW:, :] = jnp.concatenate(pieces, axis=0)
    lane = lane_index()
    even = scalar_mask(lon_parity(), 0)
    for tile in range(2):
        left = jnp.zeros((8, LANES), F32)
        right = jnp.zeros((8, LANES), F32)
        for slot in range(32 if tile == 0 else 12):
            if tile == 0:
                x = out_ref[pl.ds(slot, 8, stride=PLANE), :]
            else:
                x = out_ref[pl.ds((MEMBERS_HERE + slot // 4) * PLANE + slot % 4, 8, stride=ROWS), :]
            place = (lane // 4) == slot
            left = jnp.where(place, roll(x, 4 * slot), left)
            right = jnp.where(place, roll(x, 4 * slot + 4), right)
        first_ref[tile * 8 : tile * 8 + 8, :] = jnp.where(even, right, left)
        second_ref[tile * 8 : tile * 8 + 8, :] = jnp.where(even, left, right)


def forecast_kernel(
    own_ref, other_ref, first_ref, second_ref, corner_ref, send_ref, values_ref, coef, state
):
    lane = lane_index()
    here = lat_masks()
    even = scalar_mask(lon_parity(), 0)
    first_lane = lane == 0
    last_lane = lane == LANES - 1
    east_lanes = lane < 4
    west_lanes = lane >= LANES - 4
    east, west = {}, {}
    for block in range(2):
        for tile in range(2):
            part = slice(tile * 8, tile * 8 + 8)
            far = slice(EDGE_ROW + tile * 8, EDGE_ROW + tile * 8 + 8)
            a = jnp.where(here[block], first_ref[part, :], other_ref[far, :])
            b = jnp.where(here[block], second_ref[part, :], corner_ref[part, :])
            east[block, tile] = jnp.where(even, a, b)
            west[block, tile] = jnp.where(even, b, a)

    def halo(row, tile, group):
        slot = group * ROWS + row % ROWS
        key = (row // ROWS, tile)
        from_east = roll(east[key], -4 * slot)
        from_west = roll(west[key], LANES - 4 - 4 * slot)
        return jnp.where(east_lanes, from_east, jnp.where(west_lanes, from_west, 0.0))

    for row in range(8):
        for part in range(2):
            if part == 0:
                u, v, d = (coef_rows(own_ref, other_ref, here, q, row) for q in range(3))
            else:
                u, v, d = (halo(row, 1, q) for q in range(3))
            up, un = jnp.maximum(u, 0.0), jnp.minimum(u, 0.0)
            vp, vn = jnp.maximum(v, 0.0), jnp.minimum(v, 0.0)
            coef[row, 0, part] = 1.0 - (up - un) - (vp - vn) - 4.0 * d
            coef[row, 1, part] = up + d
            coef[row, 2, part] = d - un
            coef[row, 3, part] = vp + d
            coef[row, 4, part] = d - vn

    for level in range(LEVELS):
        q = []
        for row in range(8):
            q.append((member_rows(own_ref, other_ref, here, level, row), halo(row, 0, level)))
        for _ in range(STEPS):
            after = []
            for row in range(8):
                centre, border = q[row]
                rc, rb = roll(centre, 1), roll(border, 1)
                lc, lb = roll(centre, -1), roll(border, -1)
                wests = (jnp.where(first_lane, rb, rc), jnp.where(first_lane, rc, rb))
                easts = (jnp.where(last_lane, lb, lc), jnp.where(last_lane, lc, lb))
                pair = []
                for part in range(2):
                    c = [coef[row, n, part, level : level + 1, :] for n in range(5)]
                    total = c[0] * q[row][part] + c[1] * wests[part] + c[2] * easts[part]
                    if row > 0:
                        total = total + c[3] * q[row - 1][part]
                    if row < 7:
                        total = total + c[4] * q[row + 1][part]
                    pair.append(total)
                after.append(tuple(pair))
            q = after
        for row in range(8):
            state[level, row] = q[row][0]

    for block in range(2):
        site_own = jnp.concatenate(
            [own_ref[SITE_ROW : SITE_ROW + 1, :], own_ref[SITE_ROW + 1 : SITE_ROW + 2, :]], axis=1
        )
        site_other = jnp.concatenate(
            [other_ref[SITE_ROW : SITE_ROW + 1, :], other_ref[SITE_ROW + 1 : SITE_ROW + 2, :]], axis=1
        )
        mine = jnp.full((1, NOB), lax.axis_index("lat"), jnp.int32) == block
        site = jnp.where(mine, site_own, site_other).astype(jnp.int32)
        site_row = jnp.broadcast_to(site >> 7, (8, NOB))
        site_lane = jnp.broadcast_to(site & (LANES - 1), (LANES, NOB))
        pick = jnp.where(lax.broadcasted_iota(jnp.int32, (LANES, NOB), 0) == site_lane, 1.0, 0.0).astype(BF16)
        x = state[:, block * ROWS : (block + 1) * ROWS].reshape(PLANE * 8, LANES)
        x1 = x.astype(BF16)
        rest = x - x1.astype(F32)
        x2 = rest.astype(BF16)
        x3 = (rest - x2.astype(F32)).astype(BF16)
        picked = (
            jnp.dot(x3, pick, preferred_element_type=F32)
            + jnp.dot(x2, pick, preferred_element_type=F32)
            + jnp.dot(x1, pick, preferred_element_type=F32)
        )
        total = jnp.zeros((8, NOB), F32)
        for n in range(PLANE):
            total = jnp.where(site_row == n, picked[n * 8 : n * 8 + 8, :], total)
        for target in range(send_ref.shape[0]):
            send_ref[target, :, COLS + block * NOB : COLS + (block + 1) * NOB] = total

    own = jnp.concatenate([own_ref[VALUE_ROW + n : VALUE_ROW + n + 1, :] for n in range(2)], axis=1)
    other = jnp.concatenate([other_ref[VALUE_ROW + n : VALUE_ROW + n + 1, :] for n in range(2)], axis=1)
    south = jnp.full((1, NOB), lax.axis_index("lat"), jnp.int32) == 0
    values = jnp.concatenate([jnp.where(south, own, other), jnp.where(south, other, own)], axis=1)
    values_ref[...] = jnp.broadcast_to(values, (8, 2 * NOB))

    segment = lane // OWNED
    for row in range(ROWS):
        here_row = lax.axis_index("lat") * ROWS + row
        values = [state[level, here_row] for level in range(LEVELS)]
        for group in range(GROUPS):
            for half in range(2):
                total = jnp.zeros((8, LANES), F32)
                for n in range(4):
                    moved = roll(values[half * 4 + n], OWNED * (n - group))
                    total = jnp.where(segment == n, moved, total)
                send_ref[row * GROUPS + group, :, half * LANES : (half + 1) * LANES] = total


def halves(x):
    hi = x.astype(BF16)
    return hi, (x - hi.astype(F32)).astype(BF16)


def left_side(x):
    return jnp.concatenate(halves(x), axis=1)


def product(left, right):
    out = jnp.dot(left, right, preferred_element_type=F32)
    half = out.shape[1] // 2
    return out[:, :half] + out[:, half:]


def small_product(rows, halves_of_right):
    out = jnp.dot(jnp.concatenate(halves(rows), axis=0), halves_of_right, preferred_element_type=F32)
    half = out.shape[1] // 2
    return out[0:16, :half] + (out[0:16, half:] + out[16:32, :half])


def spread_kernel(recv_ref, values_ref, out_ref):
    members = recv_ref.shape[0]
    obs = recv_ref[:, COLS:]
    mean = jnp.sum(obs, axis=0, keepdims=True) / members
    out_ref[0:members, :] = obs - mean
    row = lax.broadcasted_iota(jnp.int32, (8, 2 * NOB), 0)
    out_ref[members:, :] = jnp.where(row == 0, values_ref[...] - mean, 0.0)


def fill_table(table, start, spread_ref):
    width = pl.ds(start, 2 * NOB)
    hi, lo = halves(spread_ref[0:128, :])
    table[0:128, width] = hi
    table[128:256, width] = lo
    innovation = spread_ref[128:129, :]
    first_term = innovation.astype(BF16).astype(F32)
    row = lax.broadcasted_iota(jnp.int32, (16, 2 * NOB), 0)
    extra = jnp.where(row == 0, first_term, jnp.where(row == 1, innovation - first_term, 0.0))
    table[256:272, width] = extra.astype(BF16)


def local_places(ids):
    code = ids >> 8
    lat_step = jnp.where(code >= 6, 2, jnp.where(code >= 3, 1, 0))
    lon_step = code - 3 * lat_step
    odd = jnp.full(ids.shape, lon_parity(), jnp.int32) == 1
    slot = jnp.where(odd, 2 - lon_step, lon_step)
    within = (lat_step - 1 + lax.axis_index("lat")) * NOB + (ids & (NOB - 1))
    near = jnp.where(slot == 0, FAR, within + jnp.where(slot == 2, 2 * NOB, 0))
    far = jnp.where(slot == 0, within, FAR)
    return near.astype(F32), far.astype(F32)


def own_kernel(payload_ref, ids_ref, weight_ref, own_ref, near_ref, far_ref, weight_out):
    own_ref[...] = payload_ref[0:EDGE_ROW, :]
    weight_out[...] = weight_ref[...]
    near_ref[...], far_ref[...] = local_places(ids_ref[...])


def gather_pair(table, places, first_column, blocks):
    place = lax.broadcasted_iota(jnp.int32, (NOB, LANES), 0).astype(F32).astype(BF16)
    one, zero = jnp.ones((), BF16), jnp.zeros((), BF16)
    hot = []
    for block in range(blocks):
        sides = []
        for k in range(2):
            row = places[pl.ds(first_column + k, 1), :] - float(block * NOB)
            sides.append(jnp.where(row.astype(BF16) == place, one, zero))
        hot.append(jnp.concatenate(sides, axis=1))
    both = jnp.dot(table[...], jnp.concatenate(hot, axis=0), preferred_element_type=F32)
    rows = both[0:128] + both[128:256]
    innov = both[256:257] + both[257:258]
    found = jnp.concatenate([rows, jnp.broadcast_to(innov, (8, 2 * LANES))], axis=0)
    return found[:, :LANES], found[:, LANES:]


def near_kernel(
    recv_ref, places, mine_ref, first_ref, part_ref, dev_ref, centre_ref, table
):
    members = recv_ref.shape[0]
    fill_table(table, 0, mine_ref)
    fill_table(table, 2 * NOB, first_ref)
    traces = jnp.transpose(recv_ref[:, :COLS])
    centre = jnp.sum(traces, axis=1, keepdims=True) / members
    dev_ref[...] = traces - centre
    centre_ref[...] = jnp.broadcast_to(centre, traces.shape)

    def turn(n, carry):
        for pair in range(BATCH // 2):
            c = n * BATCH + pair * 2
            left, right = gather_pair(table, places, c, 4)
            part_ref[c] = left
            part_ref[c + 1] = right
        return carry

    lax.fori_loop(0, OWNED // BATCH, turn, 0)


def columns_kernel(
    places,
    weight_ref,
    second_ref,
    part_ref,
    dev_ref,
    centre_ref,
    out_ref,
    table,
    res,
    eye,
    found,
    full,
    half_s,
    half_u,
    half_v,
    half_z,
    drives,
):
    members = 128
    scale = members - 1.0
    fill_table(table, 0, second_ref)
    i0 = lax.broadcasted_iota(jnp.int32, (members, members), 0)
    i1 = lax.broadcasted_iota(jnp.int32, (members, members), 1)
    eye[...] = jnp.where(i0 == i1, 1.0, 0.0).astype(F32)

    def put(ref, b, x):
        hi, lo = halves(x)
        ref[b, :, 0:members] = hi
        ref[b, :, members:] = lo

    def right_of(ref, b):
        top = ref[b]
        low = jnp.concatenate([ref[b, :, 0:members], jnp.zeros((members, members), BF16)], axis=1)
        return jnp.concatenate([top, low], axis=0)

    def turn(n, carry):
        base = n * BATCH
        slots = range(BATCH)
        invs = []
        for pair in range(BATCH // 2):
            for k, extra in enumerate(gather_pair(table, places, base + pair * 2, 2)):
                found[pair * 2 + k] = extra + part_ref[base + pair * 2 + k]
        for b in slots:
            pert = found[b, 0:members]
            innov = found[b, members : members + 1]
            w = weight_ref[pl.ds(base + b, 1), :]
            left = jnp.concatenate([pert * w, jnp.broadcast_to(w * innov, (16, LANES))], axis=0)
            e_hi, e_lo = halves(pert)
            right = jnp.concatenate(
                [
                    jnp.concatenate([e_hi, e_hi], axis=1),
                    jnp.concatenate([e_lo, jnp.zeros_like(e_lo)], axis=1),
                ],
                axis=0,
            )
            both = lax.dot_general(
                left_side(left), right, (((1,), (1,)), ((), ())), preferred_element_type=F32
            )
            both = both[:, :members] + both[:, members:]
            gram = both[:members]
            drives[b] = both[members : members + 8]
            norm = jnp.sum(jnp.sum(gram * gram, axis=0, keepdims=True), axis=1, keepdims=True)
            inv = 1.0 / (scale + jnp.sqrt(norm))
            invs.append(inv)
            s = (scale * eye[...] + gram) * inv
            full[b] = s
            put(half_s, b, s)
        for b in slots:
            square = product(half_s[b], right_of(half_s, b))
            s = full[b]
            put(half_u, b, square)
            put(half_v, b, 0.0625 * square - 0.5625 * s)
            full[b] = 2.25 * eye[...] - 2.4375 * s + 1.6875 * square
        for b in slots:
            put(half_z, b, full[b] + product(half_u[b], right_of(half_v, b)))
        rows = []
        for b in slots:
            x = jnp.concatenate([dev_ref[pl.ds(base + b, 8, stride=OWNED), :], drives[b]], axis=0)
            both = product(jnp.concatenate([half_s[b], left_side(x)], axis=0), right_of(half_z, b))
            put(half_u, b, both[0:members])
            rows.append(both[members:])
        for b in slots:
            put(half_s, b, product(half_u[b], right_of(half_z, b)))
        moved = [0.0625 * x for x in rows]
        for coefficient in (-0.5625, 1.6875, -2.4375, 2.25):
            moved = [coefficient * rows[b] + small_product(moved[b], half_s[b]) for b in slots]
        for b in slots:
            y = moved[b][0:8]
            shift = jnp.sum(y * moved[b][8:16], axis=1, keepdims=True) * invs[b]
            res[pl.ds(base + b, 8, stride=OWNED), :] = jnp.sqrt(scale * invs[b]) * y + shift
        return carry

    lax.fori_loop(0, OWNED // BATCH, turn, 0)
    out_ref[...] = jnp.transpose(res[...] + centre_ref[...])


def unpack_kernel(recv_ref, out_ref):
    segment = lane_index() // OWNED
    for row in range(ROWS):
        for half in range(2):
            parts = [
                recv_ref[row * GROUPS + g, :, half * LANES : (half + 1) * LANES] for g in range(GROUPS)
            ]
            for n in range(4):
                level = half * 4 + n
                total = jnp.zeros((8, LANES), F32)
                for g in range(GROUPS):
                    total = jnp.where(segment == g, roll(parts[g], OWNED * (g - n)), total)
                out_ref[pl.ds(level * ROWS + row, 8, stride=PLANE), :] = total


def call(kernel, shapes, operands, scratch=(), flops=None):
    single = not isinstance(shapes, list)
    cost = None
    if flops is not None:
        cost = pl.CostEstimate(flops=flops, bytes_accessed=1 << 22, transcendentals=0)
    return pl.pallas_call(
        kernel,
        out_shape=shapes,
        in_specs=vmem(len(operands)),
        out_specs=vmem(1)[0] if single else vmem(len(shapes)),
        scratch_shapes=list(scratch),
        compiler_params=params(),
        cost_estimate=cost,
    )(*operands)


def per_device(
    prior_sample_set,
    eastward_cfl_number,
    northward_cfl_number,
    spreading_number,
    obs_value,
    obs_site,
    neighbours,
    loc_weight,
):
    sds = functools.partial(jax.ShapeDtypeStruct, dtype=F32)
    mems = lax.axis_size("mem")
    lons = lax.axis_size("lon")
    on_chip = [(i, i ^ 1) for i in range(lons)]
    whole = 2 * lons
    off_chip, corners = [], []
    for i in range(whole):
        j = (i + 1 if i % 2 else i - 1) % whole
        off_chip.append((i % lons * 2 + i // lons, j % lons * 2 + j // lons))
        corners.append((i % lons * 2 + i // lons, j % lons * 2 + 1 - i // lons))
    off_lon = [(i, (i + 1 if i % 2 else i - 1) % lons) for i in range(lons)]

    edge = sds((EDGE_ROWS, LANES))
    payload, first, second, near_ids, weight = pl.pallas_call(
        payload_kernel,
        out_shape=[
            sds((PAYLOAD, LANES)),
            edge,
            edge,
            jax.ShapeDtypeStruct((OWNED, LANES), jnp.int32),
            sds((OWNED, LANES)),
        ],
        in_specs=[pl.BlockSpec(memory_space=pltpu.HBM)] * 8,
        out_specs=vmem(5),
        scratch_shapes=[
            pltpu.VMEM((1, NOB), F32),
            pltpu.VMEM((1, NOB), jnp.int32),
            pltpu.SemaphoreType.DMA((8,)),
        ],
        compiler_params=pltpu.CompilerParams(vmem_limit_bytes=PAYLOAD_LIMIT),
    )(
        prior_sample_set.reshape(MEMBERS_HERE * PLANE, LANES),
        eastward_cfl_number.reshape(PLANE, LANES),
        northward_cfl_number.reshape(PLANE, LANES),
        spreading_number.reshape(PLANE, LANES),
        obs_value.reshape(1, NOB),
        obs_site.reshape(1, NOB),
        neighbours.reshape(ROWS * LANES, LANES),
        loc_weight.reshape(ROWS * LANES, LANES),
    )
    first_in = lax.ppermute(first, "lon", on_chip)
    payload = lax.dynamic_update_slice(payload, first_in, (EDGE_ROW, 0))
    payload, second = lax.optimization_barrier((payload, second))
    other = lax.ppermute(payload, "lat", [(0, 1), (1, 0)])
    own, near, far, weight = call(
        own_kernel,
        [sds((EDGE_ROW, LANES))] + [sds((OWNED, LANES))] * 3,
        (payload, near_ids, weight),
        flops=1 << 20,
    )
    second_in = lax.ppermute(second, "lon", off_lon)
    corner_in = lax.ppermute(second, ("lon", "lat"), corners)
    send, values = call(
        forecast_kernel,
        [sds((mems, MEMBERS_HERE, COLS + 2 * NOB)), sds((8, 2 * NOB))],
        (own, other, first_in, second_in, corner_in),
        [pltpu.VMEM((8, 5, 2, 8, LANES), F32), pltpu.VMEM((LEVELS, 8, 8, LANES), F32)],
    )
    members = mems * MEMBERS_HERE
    got = lax.all_to_all(
        send.reshape(members, send.shape[2]), "mem", split_axis=0, concat_axis=0, tiled=True
    )
    spread = call(spread_kernel, sds((SPREAD_ROWS, 2 * NOB)), (got, values))
    spread_second = lax.ppermute(spread, ("lon", "lat"), off_chip)
    spread_first = lax.ppermute(spread, "lon", on_chip)
    part, dev, centre = call(
        near_kernel,
        [sds((OWNED, SPREAD_ROWS, LANES)), sds((COLS, members)), sds((COLS, members))],
        (got, near, spread, spread_first),
        [pltpu.VMEM((272, 4 * NOB), BF16)],
        flops=2 * OWNED * LANES * 272 * 4 * NOB,
    )
    updated = call(
        columns_kernel,
        sds((members, COLS)),
        (far, weight, spread_second, part, dev, centre),
        [
            pltpu.VMEM((272, 2 * NOB), BF16),
            pltpu.VMEM((COLS, members), F32),
            pltpu.VMEM((members, members), F32),
            pltpu.VMEM((BATCH, SPREAD_ROWS, LANES), F32),
            pltpu.VMEM((BATCH, members, members), F32),
            *[pltpu.VMEM((BATCH, members, 2 * members), BF16)] * 4,
            pltpu.VMEM((BATCH, 8, members), F32),
        ],
        flops=2 * OWNED * 7 * members * 4 * members * members,
    )
    back = lax.all_to_all(updated, "mem", split_axis=0, concat_axis=0, tiled=True)
    result = call(
        unpack_kernel,
        sds((MEMBERS_HERE * PLANE, LANES)),
        (back.reshape(mems, MEMBERS_HERE, COLS),),
    )
    return result.reshape(prior_sample_set.shape)


def solution(mesh):
    return jax.shard_map(
        per_device,
        mesh=mesh,
        in_specs=(
            P("mem", None, "lat", "lon"),
            P(None, "lat", "lon"),
            P(None, "lat", "lon"),
            P(None, "lat", "lon"),
            P("lat", "lon", None),
            P("lat", "lon", None),
            P("lat", "lon", None),
            P("lat", "lon", None),
        ),
        out_specs=P("mem", None, "lat", "lon"),
        check_vma=False,
    )
```

profile of v0, /device:TPU:1, one launch (start us, length us, event | category | flops | bytes accessed | tf_op | source)
XLA Modules:
  0.0 90.0 jit_solution(12318962149011545809)
XLA Ops:
  0.0 1.8 %shard_map.82 = (f32[376,128]{1,0:T(8,128)}, f32[16,128]{1,0:T(8,128)}, f32[16,128]{1,0:T(8,128)}, s32[32,128]{1,0:T(8,128)}, f32[32,128]{1,0:T(8,128)}) custom-call(f32[256,128]{1,0:T(8,128)} %bitcast.16, f32[32,128]{1,0:T(8,128)} %bitcast.17, f32[32,128]{1,0:T(8,128)} %bitcast.18, f32[32,128]{1,0:T(8,128)} %bitcast.19, f32[1,256]{1,0:T(1,128)} %bitcast.20, ...), custom_call_target="tpu_custom_call" | custom-call | tf_op jit(solution)/shard_map/pallas_call | solution.py:499
  1.8 8.8 %collective-permute-start = (f32[16,128]{1,0:T(8,128)}, f32[16,128]{1,0:T(8,128)S(1)}, u32[]{:S(2)}, u32[]{:S(2)}) collective-permute-start(f32[16,128]{1,0:T(8,128)} %get-tuple-element.22), channel_id=1, source_target_pairs={{0,2},{2,0},{4,6},{6,4},{8,10},{10,8},{12,14},{14,12},{16,18},{18,... | collective-permute-start | bytes 24584 | tf_op jit(solution)/shard_map/ppermute | solution.py:526
  10.6 1.0 %collective-permute-done.first_ref = f32[16,128]{1,0:T(8,128)S(1)} collective-permute-done((f32[16,128]{1,0:T(8,128)}, f32[16,128]{1,0:T(8,128)S(1)}, u32[]{:S(2)}, u32[]{:S(2)}) %collective-permute-start) | collective-permute-done | bytes 8224 | tf_op jit(solution)/shard_map/ppermute | solution.py:526
  11.6 0.6 constant_dynamic-update-slice_fusion.payload_ref
  12.2 10.1 %collective-permute-start.1 = (f32[376,128]{1,0:T(8,128)}, f32[376,128]{1,0:T(8,128)S(1)}, u32[]{:S(2)}, u32[]{:S(2)}) collective-permute-start(f32[376,128]{1,0:T(8,128)} %constant_dynamic-update-slice_fusion.payload_ref), channel_id=1, source_target_pairs={{0,1},{1,0},{2,3},{3,2},{4,5},{5,4},{6,7},{7,6},{8,9},{9,8},{10,11... | collective-permute-start | bytes 577544 | tf_op jit(solution)/shard_map/ppermute | solution.py:529
  22.3 3.2 %collective-permute-start.2 = (f32[16,128]{1,0:T(8,128)}, f32[16,128]{1,0:T(8,128)S(1)}, u32[]{:S(2)}, u32[]{:S(2)}) collective-permute-start(f32[16,128]{1,0:T(8,128)} %get-tuple-element.30), channel_id=1, source_target_pairs={{0,30},{2,4},{4,2},{6,8},{8,6},{10,12},{12,10},{14,16},{16,14},{18... | collective-permute-start | bytes 24584 | tf_op jit(solution)/shard_map/ppermute | solution.py:536
  25.4 3.2 %collective-permute-start.3 = (f32[16,128]{1,0:T(8,128)}, f32[16,128]{1,0:T(8,128)S(1)}, u32[]{:S(2)}, u32[]{:S(2)}) collective-permute-start(f32[16,128]{1,0:T(8,128)} %get-tuple-element.30), channel_id=1, source_target_pairs={{0,31},{2,5},{4,3},{6,9},{8,7},{10,13},{12,11},{14,17},{16,15},{18... | collective-permute-start | bytes 24584 | tf_op jit(solution)/shard_map/ppermute | solution.py:537
  28.7 0.0 copy-start
  28.7 0.9 %copy-done = f32[376,128]{1,0:T(8,128)S(1)} copy-done((f32[376,128]{1,0:T(8,128)S(1)}, f32[376,128]{1,0:T(8,128)}, u32[]{:S(2)}) %copy-start) | copy-done | bytes 192536
  29.6 0.0 copy-start.1
  29.6 0.7 copy-done.1
  30.3 0.0 copy-start.2
  30.3 0.7 copy-done.2
  31.1 10.4 %collective-permute-done.2.second_ref = f32[16,128]{1,0:T(8,128)S(1)} collective-permute-done((f32[16,128]{1,0:T(8,128)}, f32[16,128]{1,0:T(8,128)S(1)}, u32[]{:S(2)}, u32[]{:S(2)}) %collective-permute-start.2) | collective-permute-done | bytes 8224 | tf_op jit(solution)/shard_map/ppermute | solution.py:536
  41.4 0.0 collective-permute-done.3.corner_ref
  41.4 0.0 collective-permute-done.1.other_ref
  41.4 2.6 %shard_map.84 = (f32[16,8,768]{2,1,0:T(8,128)S(1)}, f32[8,512]{1,0:T(8,128)S(1)}) custom-call(f32[360,128]{1,0:T(8,128)S(1)} %get-tuple-element.29.own_ref, f32[376,128]{1,0:T(8,128)S(1)} %collective-permute-done.1.other_ref, f32[16,128]{1,0:T(8,128)S(1)} %collective-permute-done.first_ref, f32[16,128]{1,0:T(8,128)S(1)} %collective-permute-done.2.second_ref, ...), custom_call_target="tpu_custom_call" | custom-call | tf_op jit(solution)/shard_map/pallas_call | solution.py:465
  44.0 16.0 %all_to_all.17 = f32[16,8,768]{2,1,0:T(8,128)S(1)} all-to-all(f32[16,8,768]{2,1,0:T(8,128)S(1)} %get-tuple-element.31), channel_id=1, replica_groups=mesh['mem'=16,'lon'=16,'lat'=2] {'mem'}, dimensions={0} | all-to-all | bytes 786432 | tf_op jit(solution)/shard_map/all_to_all | solution.py:545
  60.0 3.5 %collective-permute-start.5 = (f32[136,512]{1,0:T(8,128)S(1)}, f32[136,512]{1,0:T(8,128)S(1)}, u32[]{:S(2)}, u32[]{:S(2)}) collective-permute-start(f32[136,512]{1,0:T(8,128)S(1)} %shard_map.85.mine_ref), channel_id=1, source_target_pairs={{0,2},{2,0},{4,6},{6,4},{8,10},{10,8},{12,14},{14,12},{16,18},{18,... | collective-permute-start | bytes 835592 | tf_op jit(solution)/shard_map/ppermute | solution.py:550
  63.6 1.9 %collective-permute-start.4 = (f32[136,512]{1,0:T(8,128)S(1)}, f32[136,512]{1,0:T(8,128)S(1)}, u32[]{:S(2)}, u32[]{:S(2)}) collective-permute-start(f32[136,512]{1,0:T(8,128)S(1)} %shard_map.85.mine_ref), channel_id=1, source_target_pairs={{0,31},{2,4},{4,2},{6,8},{8,6},{10,12},{12,10},{14,16},{16,14},{18... | collective-permute-start | bytes 835592 | tf_op jit(solution)/shard_map/ppermute | solution.py:549
  65.5 0.0 collective-permute-done.5.first_ref
  65.5 2.9 %shard_map.86 = (f32[32,136,128]{2,1,0:T(8,128)S(1)}, f32[256,128]{1,0:T(8,128)S(1)}, f32[256,128]{1,0:T(8,128)S(1)}) custom-call(f32[128,768]{1,0:T(8,128)S(1)} %bitcast.12, f32[32,128]{1,0:T(8,128)S(1)} %get-tuple-element.33.places, f32[136,512]{1,0:T(8,128)S(1)} %shard_map.85.mine_ref, f32[136,512]{1,0:T(8,128)S(1)} %collective-permute-done.5.first_ref), custom_call_target="tpu_custom_call" | custom-call | flops 2281701376 | bytes 4194304 | tf_op jit(solution)/shard_map/pallas_call | solution.py:465
  68.4 3.3 %collective-permute-done.4.second_ref = f32[136,512]{1,0:T(8,128)S(1)} collective-permute-done((f32[136,512]{1,0:T(8,128)S(1)}, f32[136,512]{1,0:T(8,128)S(1)}, u32[]{:S(2)}, u32[]{:S(2)}) %collective-permute-start.4) | collective-permute-done | bytes 278560 | tf_op jit(solution)/shard_map/ppermute | solution.py:549
  71.7 7.9 %shard_map.87 = f32[128,256]{1,0:T(8,128)S(1)} custom-call(f32[32,128]{1,0:T(8,128)S(1)} %get-tuple-element.27.places, f32[32,128]{1,0:T(8,128)S(1)} %get-tuple-element.28.weight_ref, f32[136,512]{1,0:T(8,128)S(1)} %collective-permute-done.4.second_ref, f32[32,136,128]{2,1,0:T(8,128)S(1)} %get-tuple-element.34.part_ref, ...), custom_call_target="tpu_custom_call" | custom-call | flops 3758096384 | bytes 4194304 | tf_op jit(solution)/shard_map/pallas_call | solution.py:465
  79.7 9.5 %all_to_all.18.recv_ref = f32[16,8,256]{2,1,0:T(8,128)S(1)} all-to-all(f32[16,8,256]{2,1,0:T(8,128)S(1)} %bitcast.13), channel_id=1, replica_groups=mesh['mem'=16,'lon'=16,'lat'=2] {'mem'}, dimensions={0} | all-to-all | bytes 262144 | tf_op jit(solution)/shard_map/all_to_all | solution.py:573
  89.1 0.8 shard_map.88
  (2 shorter events, 0.1 us)
Async XLA Ops:
  1.8 9.8 %collective-permute-start = (f32[16,128]{1,0:T(8,128)}, f32[16,128]{1,0:T(8,128)S(1)}, u32[]{:S(2)}, u32[]{:S(2)}) collective-permute-start(f32[16,128]{1,0:T(8,128)} %get-tuple-element.22), channel_id=1, source_target_pairs={{0,2},{2,0},{4,6},{6,4},{8,10},{10,8},{12,14},{14,12},{16,18},{18,... | collective-permute-start | bytes 24584 | tf_op jit(solution)/shard_map/ppermute | solution.py:526
  12.2 29.2 %collective-permute-start.1 = (f32[376,128]{1,0:T(8,128)}, f32[376,128]{1,0:T(8,128)S(1)}, u32[]{:S(2)}, u32[]{:S(2)}) collective-permute-start(f32[376,128]{1,0:T(8,128)} %constant_dynamic-update-slice_fusion.payload_ref), channel_id=1, source_target_pairs={{0,1},{1,0},{2,3},{3,2},{4,5},{5,4},{6,7},{7,6},{8,9},{9,8},{10,11... | collective-permute-start | bytes 577544 | tf_op jit(solution)/shard_map/ppermute | solution.py:529
  22.3 19.2 %collective-permute-start.2 = (f32[16,128]{1,0:T(8,128)}, f32[16,128]{1,0:T(8,128)S(1)}, u32[]{:S(2)}, u32[]{:S(2)}) collective-permute-start(f32[16,128]{1,0:T(8,128)} %get-tuple-element.30), channel_id=1, source_target_pairs={{0,30},{2,4},{4,2},{6,8},{8,6},{10,12},{12,10},{14,16},{16,14},{18... | collective-permute-start | bytes 24584 | tf_op jit(solution)/shard_map/ppermute | solution.py:536
  25.4 16.0 %collective-permute-start.3 = (f32[16,128]{1,0:T(8,128)}, f32[16,128]{1,0:T(8,128)S(1)}, u32[]{:S(2)}, u32[]{:S(2)}) collective-permute-start(f32[16,128]{1,0:T(8,128)} %get-tuple-element.30), channel_id=1, source_target_pairs={{0,31},{2,5},{4,3},{6,9},{8,7},{10,13},{12,11},{14,17},{16,15},{18... | collective-permute-start | bytes 24584 | tf_op jit(solution)/shard_map/ppermute | solution.py:537
  28.7 0.9 %copy-start = (f32[376,128]{1,0:T(8,128)S(1)}, f32[376,128]{1,0:T(8,128)}, u32[]{:S(2)}) copy-start(f32[376,128]{1,0:T(8,128)} %constant_dynamic-update-slice_fusion.payload_ref) | copy-start | bytes 577540
  29.6 0.7 copy-start.1
  30.3 0.7 copy-start.2
  60.0 5.5 %collective-permute-start.5 = (f32[136,512]{1,0:T(8,128)S(1)}, f32[136,512]{1,0:T(8,128)S(1)}, u32[]{:S(2)}, u32[]{:S(2)}) collective-permute-start(f32[136,512]{1,0:T(8,128)S(1)} %shard_map.85.mine_ref), channel_id=1, source_target_pairs={{0,2},{2,0},{4,6},{6,4},{8,10},{10,8},{12,14},{14,12},{16,18},{18,... | collective-permute-start | bytes 835592 | tf_op jit(solution)/shard_map/ppermute | solution.py:550
  63.6 8.2 %collective-permute-start.4 = (f32[136,512]{1,0:T(8,128)S(1)}, f32[136,512]{1,0:T(8,128)S(1)}, u32[]{:S(2)}, u32[]{:S(2)}) collective-permute-start(f32[136,512]{1,0:T(8,128)S(1)} %shard_map.85.mine_ref), channel_id=1, source_target_pairs={{0,31},{2,4},{4,2},{6,8},{8,6},{10,12},{12,10},{14,16},{16,14},{18... | collective-permute-start | bytes 835592 | tf_op jit(solution)/shard_map/ppermute | solution.py:549
where the time goes:
time: 90.5 us; the launch traced here: 90 us
  starting transfers between devices  30.7 us (34%)
  blocking collectives  25.4 us (28%)
  Pallas kernels  16 us (18%)
  waiting for transfers between devices  14.7 us (16%)
  local copies, waits for them, and re-layouts  2.95 us (3%)
    all_to_all x1, blocking collectives, per_device(): lax.all_to_all(send.reshape(members, send.shape[2]), 'mem', split_axis=0,...  16 us
    pallas_call x6, Pallas kernels, call(): pl.pallas_call(kernel, out_shape=shapes, in_specs=vmem(len(operands)), ou...  14.3 us
    ppermute x1, waiting for transfers between devices, per_device(): second_in = lax.ppermute(second, 'lon', off_lon)  10.4 us
    ppermute x1, starting transfers between devices, per_device(): other = lax.ppermute(payload, 'lat', [(0, 1), (1, 0)])  10.1 us
    all_to_all x1, blocking collectives, per_device(): lax.all_to_all(updated, 'mem', split_axis=0, concat_axis=0, tiled=True)  9.47 us
    ppermute x1, starting transfers between devices, per_device(): first_in = lax.ppermute(first, 'lon', on_chip)  8.79 us
    ppermute x1, starting transfers between devices, per_device(): spread_first = lax.ppermute(spread, 'lon', on_chip)  3.55 us
    ppermute x1, waiting for transfers between devices, per_device(): spread_second = lax.ppermute(spread, ('lon', 'lat'), off_chip)  3.35 us
  transfers between devices with their start and end apart: 6, of which 3 were waited for; matrix products, arithmetic and copies ran while one was open for 0% of the time, Pallas kernels for 3%

commit v1 on v0

--- a/solution.py
+++ b/solution.py
@@ -12,7 +12,7 @@
 OWNED = 32
 GROUPS = LANES // OWNED
 ROWS = 4
-BATCH = 16
+BATCH = 32
 MEMBERS_HERE = 8
 LEVELS = 8
 NOB = 256
@@ -132,6 +132,27 @@
         second_ref[tile * 8 : tile * 8 + 8, :] = jnp.where(even, left, right)
 
 
+def advance_in_time(q, coef, level, first_lane, last_lane):
+    after = []
+    for row in range(8):
+        centre, border = q[row]
+        rc, rb = roll(centre, 1), roll(border, 1)
+        lc, lb = roll(centre, -1), roll(border, -1)
+        wests = (jnp.where(first_lane, rb, rc), jnp.where(first_lane, rc, rb))
+        easts = (jnp.where(last_lane, lb, lc), jnp.where(last_lane, lc, lb))
+        both = []
+        for part in range(2):
+            c = [coef[row, n, part, level : level + 1, :] for n in range(5)]
+            total = c[0] * q[row][part] + c[1] * wests[part] + c[2] * easts[part]
+            if row > 0:
+                total = total + c[3] * q[row - 1][part]
+            if row < 7:
+                total = total + c[4] * q[row + 1][part]
+            both.append(total)
+        after.append(tuple(both))
+    return after
+
+
 def forecast_kernel(
     own_ref, other_ref, first_ref, second_ref, corner_ref, send_ref, values_ref, coef, state
 ):
@@ -173,31 +194,17 @@
             coef[row, 3, part] = vp + d
             coef[row, 4, part] = d - vn
 
-    for level in range(LEVELS):
-        q = []
-        for row in range(8):
-            q.append((member_rows(own_ref, other_ref, here, level, row), halo(row, 0, level)))
+    for level in range(0, LEVELS, 2):
+        pair = (level, level + 1)
+        q = [
+            [(member_rows(own_ref, other_ref, here, n, row), halo(row, 0, n)) for row in range(8)]
+            for n in pair
+        ]
         for _ in range(STEPS):
-            after = []
+            q = [advance_in_time(q[n], coef, pair[n], first_lane, last_lane) for n in range(2)]
+        for n in range(2):
             for row in range(8):
-                centre, border = q[row]
-                rc, rb = roll(centre, 1), roll(border, 1)
-                lc, lb = roll(centre, -1), roll(border, -1)
-                wests = (jnp.where(first_lane, rb, rc), jnp.where(first_lane, rc, rb))
-                easts = (jnp.where(last_lane, lb, lc), jnp.where(last_lane, lc, lb))
-                pair = []
-                for part in range(2):
-                    c = [coef[row, n, part, level : level + 1, :] for n in range(5)]
-                    total = c[0] * q[row][part] + c[1] * wests[part] + c[2] * easts[part]
-                    if row > 0:
-                        total = total + c[3] * q[row - 1][part]
-                    if row < 7:
-                        total = total + c[4] * q[row + 1][part]
-                    pair.append(total)
-                after.append(tuple(pair))
-            q = after
-        for row in range(8):
-            state[level, row] = q[row][0]
+                state[pair[n], row] = q[n][row][0]
 
     for block in range(2):
         site_own = jnp.concatenate(

time: 90.5 us -> 89.3 us (0.987)
  Pallas kernels: 16 us -> 14.5 us
    pallas_call x6, Pallas kernels: 14.3 us -> 12.7 us  [call(): pl.pallas_call(kernel, out_shape=shapes, in_specs=vmem(len(operands)), ou...]
where the time goes in v1:
time: 89.3 us; the launch traced here: 88.8 us
  starting transfers between devices  30.7 us (34%)
  blocking collectives  25.4 us (28%)
  waiting for transfers between devices  15.1 us (17%)
  Pallas kernels  14.5 us (16%)
  local copies, waits for them, and re-layouts  2.95 us (3%)
    all_to_all x1, blocking collectives, per_device(): lax.all_to_all(send.reshape(members, send.shape[2]), 'mem', split_axis=0,...  16 us
    pallas_call x6, Pallas kernels, call(): pl.pallas_call(kernel, out_shape=shapes, in_specs=vmem(len(operands)), ou...  12.7 us
    ppermute x1, waiting for transfers between devices, per_device(): second_in = lax.ppermute(second, 'lon', off_lon)  10.4 us
    ppermute x1, starting transfers between devices, per_device(): other = lax.ppermute(payload, 'lat', [(0, 1), (1, 0)])  10.1 us
    all_to_all x1, blocking collectives, per_device(): lax.all_to_all(updated, 'mem', split_axis=0, concat_axis=0, tiled=True)  9.46 us
    ppermute x1, starting transfers between devices, per_device(): first_in = lax.ppermute(first, 'lon', on_chip)  8.79 us
    ppermute x1, waiting for transfers between devices, per_device(): spread_second = lax.ppermute(spread, ('lon', 'lat'), off_chip)  3.74 us
    ppermute x1, starting transfers between devices, per_device(): spread_first = lax.ppermute(spread, 'lon', on_chip)  3.54 us
  transfers between devices with their start and end apart: 6, of which 3 were waited for; matrix products, arithmetic and copies ran while one was open for 0% of the time, Pallas kernels for 3%

profile of v1, /device:TPU:1, one launch (start us, length us, event | category | flops | bytes accessed | tf_op | source)
XLA Modules:
  0.0 88.8 jit_solution(15133230315055436991)
XLA Ops:
  0.0 1.8 %shard_map.82 = (f32[376,128]{1,0:T(8,128)}, f32[16,128]{1,0:T(8,128)}, f32[16,128]{1,0:T(8,128)}, s32[32,128]{1,0:T(8,128)}, f32[32,128]{1,0:T(8,128)}) custom-call(f32[256,128]{1,0:T(8,128)} %bitcast.16, f32[32,128]{1,0:T(8,128)} %bitcast.17, f32[32,128]{1,0:T(8,128)} %bitcast.18, f32[32,128]{1,0:T(8,128)} %bitcast.19, f32[1,256]{1,0:T(1,128)} %bitcast.20, ...), custom_call_target="tpu_custom_call" | custom-call | tf_op jit(solution)/shard_map/pallas_call | solution.py:506
  1.8 8.8 %collective-permute-start = (f32[16,128]{1,0:T(8,128)}, f32[16,128]{1,0:T(8,128)S(1)}, u32[]{:S(2)}, u32[]{:S(2)}) collective-permute-start(f32[16,128]{1,0:T(8,128)} %get-tuple-element.22), channel_id=1, source_target_pairs={{0,2},{2,0},{4,6},{6,4},{8,10},{10,8},{12,14},{14,12},{16,18},{18,... | collective-permute-start | bytes 24584 | tf_op jit(solution)/shard_map/ppermute | solution.py:533
  10.6 1.0 %collective-permute-done.first_ref = f32[16,128]{1,0:T(8,128)S(1)} collective-permute-done((f32[16,128]{1,0:T(8,128)}, f32[16,128]{1,0:T(8,128)S(1)}, u32[]{:S(2)}, u32[]{:S(2)}) %collective-permute-start) | collective-permute-done | bytes 8224 | tf_op jit(solution)/shard_map/ppermute | solution.py:533
  11.6 0.6 constant_dynamic-update-slice_fusion.payload_ref
  12.2 10.1 %collective-permute-start.1 = (f32[376,128]{1,0:T(8,128)}, f32[376,128]{1,0:T(8,128)S(1)}, u32[]{:S(2)}, u32[]{:S(2)}) collective-permute-start(f32[376,128]{1,0:T(8,128)} %constant_dynamic-update-slice_fusion.payload_ref), channel_id=1, source_target_pairs={{0,1},{1,0},{2,3},{3,2},{4,5},{5,4},{6,7},{7,6},{8,9},{9,8},{10,11... | collective-permute-start | bytes 577544 | tf_op jit(solution)/shard_map/ppermute | solution.py:536
  22.3 3.2 %collective-permute-start.2 = (f32[16,128]{1,0:T(8,128)}, f32[16,128]{1,0:T(8,128)S(1)}, u32[]{:S(2)}, u32[]{:S(2)}) collective-permute-start(f32[16,128]{1,0:T(8,128)} %get-tuple-element.30), channel_id=1, source_target_pairs={{0,30},{2,4},{4,2},{6,8},{8,6},{10,12},{12,10},{14,16},{16,14},{18... | collective-permute-start | bytes 24584 | tf_op jit(solution)/shard_map/ppermute | solution.py:543
  25.4 3.2 %collective-permute-start.3 = (f32[16,128]{1,0:T(8,128)}, f32[16,128]{1,0:T(8,128)S(1)}, u32[]{:S(2)}, u32[]{:S(2)}) collective-permute-start(f32[16,128]{1,0:T(8,128)} %get-tuple-element.30), channel_id=1, source_target_pairs={{0,31},{2,5},{4,3},{6,9},{8,7},{10,13},{12,11},{14,17},{16,15},{18... | collective-permute-start | bytes 24584 | tf_op jit(solution)/shard_map/ppermute | solution.py:544
  28.7 0.0 copy-start
  28.7 0.9 %copy-done = f32[376,128]{1,0:T(8,128)S(1)} copy-done((f32[376,128]{1,0:T(8,128)S(1)}, f32[376,128]{1,0:T(8,128)}, u32[]{:S(2)}) %copy-start) | copy-done | bytes 192536
  29.6 0.0 copy-start.1
  29.6 0.7 copy-done.1
  30.3 0.0 copy-start.2
  30.3 0.7 copy-done.2
  31.1 10.4 %collective-permute-done.2.second_ref = f32[16,128]{1,0:T(8,128)S(1)} collective-permute-done((f32[16,128]{1,0:T(8,128)}, f32[16,128]{1,0:T(8,128)S(1)}, u32[]{:S(2)}, u32[]{:S(2)}) %collective-permute-start.2) | collective-permute-done | bytes 8224 | tf_op jit(solution)/shard_map/ppermute | solution.py:543
  41.4 0.0 collective-permute-done.3.corner_ref
  41.4 0.0 collective-permute-done.1.other_ref
  41.4 1.9 %shard_map.84 = (f32[16,8,768]{2,1,0:T(8,128)S(1)}, f32[8,512]{1,0:T(8,128)S(1)}) custom-call(f32[360,128]{1,0:T(8,128)S(1)} %get-tuple-element.29.own_ref, f32[376,128]{1,0:T(8,128)S(1)} %collective-permute-done.1.other_ref, f32[16,128]{1,0:T(8,128)S(1)} %collective-permute-done.first_ref, f32[16,128]{1,0:T(8,128)S(1)} %collective-permute-done.2.second_ref, ...), custom_call_target="tpu_custom_call" | custom-call | tf_op jit(solution)/shard_map/pallas_call | solution.py:472
  43.3 16.0 %all_to_all.17 = f32[16,8,768]{2,1,0:T(8,128)S(1)} all-to-all(f32[16,8,768]{2,1,0:T(8,128)S(1)} %get-tuple-element.31), channel_id=1, replica_groups=mesh['mem'=16,'lon'=16,'lat'=2] {'mem'}, dimensions={0} | all-to-all | bytes 786432 | tf_op jit(solution)/shard_map/all_to_all | solution.py:552
  59.3 3.5 %collective-permute-start.5 = (f32[136,512]{1,0:T(8,128)S(1)}, f32[136,512]{1,0:T(8,128)S(1)}, u32[]{:S(2)}, u32[]{:S(2)}) collective-permute-start(f32[136,512]{1,0:T(8,128)S(1)} %shard_map.85.mine_ref), channel_id=1, source_target_pairs={{0,2},{2,0},{4,6},{6,4},{8,10},{10,8},{12,14},{14,12},{16,18},{18,... | collective-permute-start | bytes 835592 | tf_op jit(solution)/shard_map/ppermute | solution.py:557
  62.9 1.9 %collective-permute-start.4 = (f32[136,512]{1,0:T(8,128)S(1)}, f32[136,512]{1,0:T(8,128)S(1)}, u32[]{:S(2)}, u32[]{:S(2)}) collective-permute-start(f32[136,512]{1,0:T(8,128)S(1)} %shard_map.85.mine_ref), channel_id=1, source_target_pairs={{0,31},{2,4},{4,2},{6,8},{8,6},{10,12},{12,10},{14,16},{16,14},{18... | collective-permute-start | bytes 835592 | tf_op jit(solution)/shard_map/ppermute | solution.py:556
  64.8 0.0 collective-permute-done.5.first_ref
  64.8 2.5 %shard_map.86 = (f32[32,136,128]{2,1,0:T(8,128)S(1)}, f32[256,128]{1,0:T(8,128)S(1)}, f32[256,128]{1,0:T(8,128)S(1)}) custom-call(f32[128,768]{1,0:T(8,128)S(1)} %bitcast.12, f32[32,128]{1,0:T(8,128)S(1)} %get-tuple-element.33.places, f32[136,512]{1,0:T(8,128)S(1)} %shard_map.85.mine_ref, f32[136,512]{1,0:T(8,128)S(1)} %collective-permute-done.5.first_ref), custom_call_target="tpu_custom_call" | custom-call | flops 2281701376 | bytes 4194304 | tf_op jit(solution)/shard_map/pallas_call | solution.py:472
  67.3 3.7 %collective-permute-done.4.second_ref = f32[136,512]{1,0:T(8,128)S(1)} collective-permute-done((f32[136,512]{1,0:T(8,128)S(1)}, f32[136,512]{1,0:T(8,128)S(1)}, u32[]{:S(2)}, u32[]{:S(2)}) %collective-permute-start.4) | collective-permute-done | bytes 278560 | tf_op jit(solution)/shard_map/ppermute | solution.py:556
  71.0 7.4 %shard_map.87 = f32[128,256]{1,0:T(8,128)S(1)} custom-call(f32[32,128]{1,0:T(8,128)S(1)} %get-tuple-element.27.places, f32[32,128]{1,0:T(8,128)S(1)} %get-tuple-element.28.weight_ref, f32[136,512]{1,0:T(8,128)S(1)} %collective-permute-done.4.second_ref, f32[32,136,128]{2,1,0:T(8,128)S(1)} %get-tuple-element.34.part_ref, ...), custom_call_target="tpu_custom_call" | custom-call | flops 3758096384 | bytes 4194304 | tf_op jit(solution)/shard_map/pallas_call | solution.py:472
  78.5 9.5 %all_to_all.18.recv_ref = f32[16,8,256]{2,1,0:T(8,128)S(1)} all-to-all(f32[16,8,256]{2,1,0:T(8,128)S(1)} %bitcast.13), channel_id=1, replica_groups=mesh['mem'=16,'lon'=16,'lat'=2] {'mem'}, dimensions={0} | all-to-all | bytes 262144 | tf_op jit(solution)/shard_map/all_to_all | solution.py:580
  87.9 0.8 shard_map.88
  (2 shorter events, 0.1 us)
Async XLA Ops:
  1.8 9.8 %collective-permute-start = (f32[16,128]{1,0:T(8,128)}, f32[16,128]{1,0:T(8,128)S(1)}, u32[]{:S(2)}, u32[]{:S(2)}) collective-permute-start(f32[16,128]{1,0:T(8,128)} %get-tuple-element.22), channel_id=1, source_target_pairs={{0,2},{2,0},{4,6},{6,4},{8,10},{10,8},{12,14},{14,12},{16,18},{18,... | collective-permute-start | bytes 24584 | tf_op jit(solution)/shard_map/ppermute | solution.py:533
  12.2 29.2 %collective-permute-start.1 = (f32[376,128]{1,0:T(8,128)}, f32[376,128]{1,0:T(8,128)S(1)}, u32[]{:S(2)}, u32[]{:S(2)}) collective-permute-start(f32[376,128]{1,0:T(8,128)} %constant_dynamic-update-slice_fusion.payload_ref), channel_id=1, source_target_pairs={{0,1},{1,0},{2,3},{3,2},{4,5},{5,4},{6,7},{7,6},{8,9},{9,8},{10,11... | collective-permute-start | bytes 577544 | tf_op jit(solution)/shard_map/ppermute | solution.py:536
  22.3 19.2 %collective-permute-start.2 = (f32[16,128]{1,0:T(8,128)}, f32[16,128]{1,0:T(8,128)S(1)}, u32[]{:S(2)}, u32[]{:S(2)}) collective-permute-start(f32[16,128]{1,0:T(8,128)} %get-tuple-element.30), channel_id=1, source_target_pairs={{0,30},{2,4},{4,2},{6,8},{8,6},{10,12},{12,10},{14,16},{16,14},{18... | collective-permute-start | bytes 24584 | tf_op jit(solution)/shard_map/ppermute | solution.py:543
  25.4 16.0 %collective-permute-start.3 = (f32[16,128]{1,0:T(8,128)}, f32[16,128]{1,0:T(8,128)S(1)}, u32[]{:S(2)}, u32[]{:S(2)}) collective-permute-start(f32[16,128]{1,0:T(8,128)} %get-tuple-element.30), channel_id=1, source_target_pairs={{0,31},{2,5},{4,3},{6,9},{8,7},{10,13},{12,11},{14,17},{16,15},{18... | collective-permute-start | bytes 24584 | tf_op jit(solution)/shard_map/ppermute | solution.py:544
  28.7 0.9 %copy-start = (f32[376,128]{1,0:T(8,128)S(1)}, f32[376,128]{1,0:T(8,128)}, u32[]{:S(2)}) copy-start(f32[376,128]{1,0:T(8,128)} %constant_dynamic-update-slice_fusion.payload_ref) | copy-start | bytes 577540
  29.6 0.7 copy-start.1
  30.3 0.7 copy-start.2
  59.3 5.5 %collective-permute-start.5 = (f32[136,512]{1,0:T(8,128)S(1)}, f32[136,512]{1,0:T(8,128)S(1)}, u32[]{:S(2)}, u32[]{:S(2)}) collective-permute-start(f32[136,512]{1,0:T(8,128)S(1)} %shard_map.85.mine_ref), channel_id=1, source_target_pairs={{0,2},{2,0},{4,6},{6,4},{8,10},{10,8},{12,14},{14,12},{16,18},{18,... | collective-permute-start | bytes 835592 | tf_op jit(solution)/shard_map/ppermute | solution.py:557
  62.9 8.2 %collective-permute-start.4 = (f32[136,512]{1,0:T(8,128)S(1)}, f32[136,512]{1,0:T(8,128)S(1)}, u32[]{:S(2)}, u32[]{:S(2)}) collective-permute-start(f32[136,512]{1,0:T(8,128)S(1)} %shard_map.85.mine_ref), channel_id=1, source_target_pairs={{0,31},{2,4},{4,2},{6,8},{8,6},{10,12},{12,10},{14,16},{16,14},{18... | collective-permute-start | bytes 835592 | tf_op jit(solution)/shard_map/ppermute | solution.py:556

commit v2 on v1

--- a/solution.py
+++ b/solution.py
@@ -154,7 +154,7 @@
 
 
 def forecast_kernel(
-    own_ref, other_ref, first_ref, second_ref, corner_ref, send_ref, values_ref, coef, state
+    own_ref, other_ref, corner_ref, second_ref, first_ref, send_ref, values_ref, coef, state
 ):
     lane = lane_index()
     here = lat_masks()
@@ -400,18 +400,15 @@
             innov = found[b, members : members + 1]
             w = weight_ref[pl.ds(base + b, 1), :]
             left = jnp.concatenate([pert * w, jnp.broadcast_to(w * innov, (16, LANES))], axis=0)
-            e_hi, e_lo = halves(pert)
+            e_hi, e_lo = halves(jnp.transpose(pert))
             right = jnp.concatenate(
                 [
-                    jnp.concatenate([e_hi, e_hi], axis=1),
-                    jnp.concatenate([e_lo, jnp.zeros_like(e_lo)], axis=1),
+                    jnp.concatenate([e_hi, e_lo], axis=1),
+                    jnp.concatenate([e_hi, jnp.zeros_like(e_hi)], axis=1),
                 ],
                 axis=0,
             )
-            both = lax.dot_general(
-                left_side(left), right, (((1,), (1,)), ((), ())), preferred_element_type=F32
-            )
-            both = both[:, :members] + both[:, members:]
+            both = product(left_side(left), right)
             gram = both[:members]
             drives[b] = both[members : members + 8]
             norm = jnp.sum(jnp.sum(gram * gram, axis=0, keepdims=True), axis=1, keepdims=True)
@@ -540,12 +537,12 @@
         (payload, near_ids, weight),
         flops=1 << 20,
     )
+    corner_in = lax.ppermute(second, ("lon", "lat"), corners)
     second_in = lax.ppermute(second, "lon", off_lon)
-    corner_in = lax.ppermute(second, ("lon", "lat"), corners)
     send, values = call(
         forecast_kernel,
         [sds((mems, MEMBERS_HERE, COLS + 2 * NOB)), sds((8, 2 * NOB))],
-        (own, other, first_in, second_in, corner_in),
+        (own, other, corner_in, second_in, first_in),
         [pltpu.VMEM((8, 5, 2, 8, LANES), F32), pltpu.VMEM((LEVELS, 8, 8, LANES), F32)],
     )
     members = mems * MEMBERS_HERE

time: 89.3 us -> 89.4 us (level)
    ppermute x1, waiting for transfers between devices: 10.4 us -> 5.36 us  [per_device(): second_in = lax.ppermute(second, 'lon', off_lon)]
    ppermute x1, waiting for transfers between devices: 0.01 us -> 4.99 us  [per_device(): corner_in = lax.ppermute(second, ('lon', 'lat'), corners)]
    ppermute x1, starting transfers between devices: 3.16 us -> 4.48 us  [per_device(): second_in = lax.ppermute(second, 'lon', off_lon)]
    ppermute x1, starting transfers between devices: 3.24 us -> 1.92 us  [per_device(): corner_in = lax.ppermute(second, ('lon', 'lat'), corners)]
  transfers between devices with their start and end apart: 6 -> 6, of which waited for: 3 -> 4; matrix products, arithmetic and copies ran while one was open for 0% -> 0% of each run, Pallas kernels for 3% -> 3%
where the time goes in v2:
time: 89.4 us; the launch traced here: 88.6 us
  starting transfers between devices  30.7 us (34%)
  blocking collectives  25.4 us (28%)
  waiting for transfers between devices  15.1 us (17%)
  Pallas kernels  14.3 us (16%)
  local copies, waits for them, and re-layouts  2.95 us (3%)
    all_to_all x1, blocking collectives, per_device(): lax.all_to_all(send.reshape(members, send.shape[2]), 'mem', split_axis=0,...  15.9 us
    pallas_call x6, Pallas kernels, call(): pl.pallas_call(kernel, out_shape=shapes, in_specs=vmem(len(operands)), ou...  12.5 us
    ppermute x1, starting transfers between devices, per_device(): other = lax.ppermute(payload, 'lat', [(0, 1), (1, 0)])  10.1 us
    all_to_all x1, blocking collectives, per_device(): lax.all_to_all(updated, 'mem', split_axis=0, concat_axis=0, tiled=True)  9.46 us
    ppermute x1, starting transfers between devices, per_device(): first_in = lax.ppermute(first, 'lon', on_chip)  8.79 us
    ppermute x1, waiting for transfers between devices, per_device(): second_in = lax.ppermute(second, 'lon', off_lon)  5.36 us
    ppermute x1, waiting for transfers between devices, per_device(): corner_in = lax.ppermute(second, ('lon', 'lat'), corners)  4.99 us
    ppermute x1, starting transfers between devices, per_device(): second_in = lax.ppermute(second, 'lon', off_lon)  4.48 us
  transfers between devices with their start and end apart: 6, of which 4 were waited for; matrix products, arithmetic and copies ran while one was open for 0% of the time, Pallas kernels for 3%

profile of v2, /device:TPU:1, one launch (start us, length us, event | category | flops | bytes accessed | tf_op | source)
XLA Modules:
  0.0 88.6 jit_solution(6789798689535552199)
XLA Ops:
  0.0 1.8 %shard_map.82 = (f32[376,128]{1,0:T(8,128)}, f32[16,128]{1,0:T(8,128)}, f32[16,128]{1,0:T(8,128)}, s32[32,128]{1,0:T(8,128)}, f32[32,128]{1,0:T(8,128)}) custom-call(f32[256,128]{1,0:T(8,128)} %bitcast.16, f32[32,128]{1,0:T(8,128)} %bitcast.17, f32[32,128]{1,0:T(8,128)} %bitcast.18, f32[32,128]{1,0:T(8,128)} %bitcast.19, f32[1,256]{1,0:T(1,128)} %bitcast.20, ...), custom_call_target="tpu_custom_call" | custom-call | tf_op jit(solution)/shard_map/pallas_call | solution.py:503
  1.8 8.8 %collective-permute-start = (f32[16,128]{1,0:T(8,128)}, f32[16,128]{1,0:T(8,128)S(1)}, u32[]{:S(2)}, u32[]{:S(2)}) collective-permute-start(f32[16,128]{1,0:T(8,128)} %get-tuple-element.22), channel_id=1, source_target_pairs={{0,2},{2,0},{4,6},{6,4},{8,10},{10,8},{12,14},{14,12},{16,18},{18,... | collective-permute-start | bytes 24584 | tf_op jit(solution)/shard_map/ppermute | solution.py:530
  10.6 1.0 %collective-permute-done.first_ref = f32[16,128]{1,0:T(8,128)S(1)} collective-permute-done((f32[16,128]{1,0:T(8,128)}, f32[16,128]{1,0:T(8,128)S(1)}, u32[]{:S(2)}, u32[]{:S(2)}) %collective-permute-start) | collective-permute-done | bytes 8224 | tf_op jit(solution)/shard_map/ppermute | solution.py:530
  11.6 0.6 constant_dynamic-update-slice_fusion.payload_ref
  12.2 10.1 %collective-permute-start.1 = (f32[376,128]{1,0:T(8,128)}, f32[376,128]{1,0:T(8,128)S(1)}, u32[]{:S(2)}, u32[]{:S(2)}) collective-permute-start(f32[376,128]{1,0:T(8,128)} %constant_dynamic-update-slice_fusion.payload_ref), channel_id=1, source_target_pairs={{0,1},{1,0},{2,3},{3,2},{4,5},{5,4},{6,7},{7,6},{8,9},{9,8},{10,11... | collective-permute-start | bytes 577544 | tf_op jit(solution)/shard_map/ppermute | solution.py:533
  22.3 1.9 %collective-permute-start.2 = (f32[16,128]{1,0:T(8,128)}, f32[16,128]{1,0:T(8,128)S(1)}, u32[]{:S(2)}, u32[]{:S(2)}) collective-permute-start(f32[16,128]{1,0:T(8,128)} %get-tuple-element.30), channel_id=1, source_target_pairs={{0,31},{2,5},{4,3},{6,9},{8,7},{10,13},{12,11},{14,17},{16,15},{18... | collective-permute-start | bytes 24584 | tf_op jit(solution)/shard_map/ppermute | solution.py:540
  24.2 4.5 %collective-permute-start.3 = (f32[16,128]{1,0:T(8,128)}, f32[16,128]{1,0:T(8,128)S(1)}, u32[]{:S(2)}, u32[]{:S(2)}) collective-permute-start(f32[16,128]{1,0:T(8,128)} %get-tuple-element.30), channel_id=1, source_target_pairs={{0,30},{2,4},{4,2},{6,8},{8,6},{10,12},{12,10},{14,16},{16,14},{18... | collective-permute-start | bytes 24584 | tf_op jit(solution)/shard_map/ppermute | solution.py:541
  28.7 0.0 copy-start
  28.7 0.9 %copy-done = f32[376,128]{1,0:T(8,128)S(1)} copy-done((f32[376,128]{1,0:T(8,128)S(1)}, f32[376,128]{1,0:T(8,128)}, u32[]{:S(2)}) %copy-start) | copy-done | bytes 192536
  29.6 0.0 copy-start.1
  29.6 0.7 copy-done.1
  30.3 0.0 copy-start.2
  30.3 0.7 copy-done.2
  31.1 5.0 %collective-permute-done.2.corner_ref = f32[16,128]{1,0:T(8,128)S(1)} collective-permute-done((f32[16,128]{1,0:T(8,128)}, f32[16,128]{1,0:T(8,128)S(1)}, u32[]{:S(2)}, u32[]{:S(2)}) %collective-permute-start.2) | collective-permute-done | bytes 8224 | tf_op jit(solution)/shard_map/ppermute | solution.py:540
  36.1 5.4 %collective-permute-done.3.second_ref = f32[16,128]{1,0:T(8,128)S(1)} collective-permute-done((f32[16,128]{1,0:T(8,128)}, f32[16,128]{1,0:T(8,128)S(1)}, u32[]{:S(2)}, u32[]{:S(2)}) %collective-permute-start.3) | collective-permute-done | bytes 8224 | tf_op jit(solution)/shard_map/ppermute | solution.py:541
  41.4 0.0 collective-permute-done.1.other_ref
  41.4 1.9 %shard_map.84 = (f32[16,8,768]{2,1,0:T(8,128)S(1)}, f32[8,512]{1,0:T(8,128)S(1)}) custom-call(f32[360,128]{1,0:T(8,128)S(1)} %get-tuple-element.29.own_ref, f32[376,128]{1,0:T(8,128)S(1)} %collective-permute-done.1.other_ref, f32[16,128]{1,0:T(8,128)S(1)} %collective-permute-done.2.corner_ref, f32[16,128]{1,0:T(8,128)S(1)} %collective-permute-done.3.second_ref, ...), custom_call_target="tpu_custom_call" | custom-call | tf_op jit(solution)/shard_map/pallas_call | solution.py:469
  43.3 15.9 %all_to_all.17 = f32[16,8,768]{2,1,0:T(8,128)S(1)} all-to-all(f32[16,8,768]{2,1,0:T(8,128)S(1)} %get-tuple-element.31), channel_id=1, replica_groups=mesh['mem'=16,'lon'=16,'lat'=2] {'mem'}, dimensions={0} | all-to-all | bytes 786432 | tf_op jit(solution)/shard_map/all_to_all | solution.py:549
  59.3 3.6 %collective-permute-start.5 = (f32[136,512]{1,0:T(8,128)S(1)}, f32[136,512]{1,0:T(8,128)S(1)}, u32[]{:S(2)}, u32[]{:S(2)}) collective-permute-start(f32[136,512]{1,0:T(8,128)S(1)} %shard_map.85.mine_ref), channel_id=1, source_target_pairs={{0,2},{2,0},{4,6},{6,4},{8,10},{10,8},{12,14},{14,12},{16,18},{18,... | collective-permute-start | bytes 835592 | tf_op jit(solution)/shard_map/ppermute | solution.py:554
  62.9 1.9 %collective-permute-start.4 = (f32[136,512]{1,0:T(8,128)S(1)}, f32[136,512]{1,0:T(8,128)S(1)}, u32[]{:S(2)}, u32[]{:S(2)}) collective-permute-start(f32[136,512]{1,0:T(8,128)S(1)} %shard_map.85.mine_ref), channel_id=1, source_target_pairs={{0,31},{2,4},{4,2},{6,8},{8,6},{10,12},{12,10},{14,16},{16,14},{18... | collective-permute-start | bytes 835592 | tf_op jit(solution)/shard_map/ppermute | solution.py:553
  64.8 0.0 collective-permute-done.5.first_ref
  64.8 2.5 %shard_map.86 = (f32[32,136,128]{2,1,0:T(8,128)S(1)}, f32[256,128]{1,0:T(8,128)S(1)}, f32[256,128]{1,0:T(8,128)S(1)}) custom-call(f32[128,768]{1,0:T(8,128)S(1)} %bitcast.12, f32[32,128]{1,0:T(8,128)S(1)} %get-tuple-element.33.places, f32[136,512]{1,0:T(8,128)S(1)} %shard_map.85.mine_ref, f32[136,512]{1,0:T(8,128)S(1)} %collective-permute-done.5.first_ref), custom_call_target="tpu_custom_call" | custom-call | flops 2281701376 | bytes 4194304 | tf_op jit(solution)/shard_map/pallas_call | solution.py:469
  67.3 3.7 %collective-permute-done.4.second_ref = f32[136,512]{1,0:T(8,128)S(1)} collective-permute-done((f32[136,512]{1,0:T(8,128)S(1)}, f32[136,512]{1,0:T(8,128)S(1)}, u32[]{:S(2)}, u32[]{:S(2)}) %collective-permute-start.4) | collective-permute-done | bytes 278560 | tf_op jit(solution)/shard_map/ppermute | solution.py:553
  71.0 7.2 %shard_map.87 = f32[128,256]{1,0:T(8,128)S(1)} custom-call(f32[32,128]{1,0:T(8,128)S(1)} %get-tuple-element.27.places, f32[32,128]{1,0:T(8,128)S(1)} %get-tuple-element.28.weight_ref, f32[136,512]{1,0:T(8,128)S(1)} %collective-permute-done.4.second_ref, f32[32,136,128]{2,1,0:T(8,128)S(1)} %get-tuple-element.34.part_ref, ...), custom_call_target="tpu_custom_call" | custom-call | flops 3758096384 | bytes 4194304 | tf_op jit(solution)/shard_map/pallas_call | solution.py:469
  78.3 9.5 %all_to_all.18.recv_ref = f32[16,8,256]{2,1,0:T(8,128)S(1)} all-to-all(f32[16,8,256]{2,1,0:T(8,128)S(1)} %bitcast.13), channel_id=1, replica_groups=mesh['mem'=16,'lon'=16,'lat'=2] {'mem'}, dimensions={0} | all-to-all | bytes 262144 | tf_op jit(solution)/shard_map/all_to_all | solution.py:577
  87.7 0.8 shard_map.88
  (2 shorter events, 0.1 us)
Async XLA Ops:
  1.8 9.8 %collective-permute-start = (f32[16,128]{1,0:T(8,128)}, f32[16,128]{1,0:T(8,128)S(1)}, u32[]{:S(2)}, u32[]{:S(2)}) collective-permute-start(f32[16,128]{1,0:T(8,128)} %get-tuple-element.22), channel_id=1, source_target_pairs={{0,2},{2,0},{4,6},{6,4},{8,10},{10,8},{12,14},{14,12},{16,18},{18,... | collective-permute-start | bytes 24584 | tf_op jit(solution)/shard_map/ppermute | solution.py:530
  12.2 29.2 %collective-permute-start.1 = (f32[376,128]{1,0:T(8,128)}, f32[376,128]{1,0:T(8,128)S(1)}, u32[]{:S(2)}, u32[]{:S(2)}) collective-permute-start(f32[376,128]{1,0:T(8,128)} %constant_dynamic-update-slice_fusion.payload_ref), channel_id=1, source_target_pairs={{0,1},{1,0},{2,3},{3,2},{4,5},{5,4},{6,7},{7,6},{8,9},{9,8},{10,11... | collective-permute-start | bytes 577544 | tf_op jit(solution)/shard_map/ppermute | solution.py:533
  22.3 13.8 %collective-permute-start.2 = (f32[16,128]{1,0:T(8,128)}, f32[16,128]{1,0:T(8,128)S(1)}, u32[]{:S(2)}, u32[]{:S(2)}) collective-permute-start(f32[16,128]{1,0:T(8,128)} %get-tuple-element.30), channel_id=1, source_target_pairs={{0,31},{2,5},{4,3},{6,9},{8,7},{10,13},{12,11},{14,17},{16,15},{18... | collective-permute-start | bytes 24584 | tf_op jit(solution)/shard_map/ppermute | solution.py:540
  24.2 17.2 %collective-permute-start.3 = (f32[16,128]{1,0:T(8,128)}, f32[16,128]{1,0:T(8,128)S(1)}, u32[]{:S(2)}, u32[]{:S(2)}) collective-permute-start(f32[16,128]{1,0:T(8,128)} %get-tuple-element.30), channel_id=1, source_target_pairs={{0,30},{2,4},{4,2},{6,8},{8,6},{10,12},{12,10},{14,16},{16,14},{18... | collective-permute-start | bytes 24584 | tf_op jit(solution)/shard_map/ppermute | solution.py:541
  28.7 0.9 %copy-start = (f32[376,128]{1,0:T(8,128)S(1)}, f32[376,128]{1,0:T(8,128)}, u32[]{:S(2)}) copy-start(f32[376,128]{1,0:T(8,128)} %constant_dynamic-update-slice_fusion.payload_ref) | copy-start | bytes 577540
  29.6 0.7 copy-start.1
  30.3 0.7 copy-start.2
  59.3 5.5 %collective-permute-start.5 = (f32[136,512]{1,0:T(8,128)S(1)}, f32[136,512]{1,0:T(8,128)S(1)}, u32[]{:S(2)}, u32[]{:S(2)}) collective-permute-start(f32[136,512]{1,0:T(8,128)S(1)} %shard_map.85.mine_ref), channel_id=1, source_target_pairs={{0,2},{2,0},{4,6},{6,4},{8,10},{10,8},{12,14},{14,12},{16,18},{18,... | collective-permute-start | bytes 835592 | tf_op jit(solution)/shard_map/ppermute | solution.py:554
  62.9 8.2 %collective-permute-start.4 = (f32[136,512]{1,0:T(8,128)S(1)}, f32[136,512]{1,0:T(8,128)S(1)}, u32[]{:S(2)}, u32[]{:S(2)}) collective-permute-start(f32[136,512]{1,0:T(8,128)S(1)} %shard_map.85.mine_ref), channel_id=1, source_target_pairs={{0,31},{2,4},{4,2},{6,8},{8,6},{10,12},{12,10},{14,16},{16,14},{18... | collective-permute-start | bytes 835592 | tf_op jit(solution)/shard_map/ppermute | solution.py:553

commit v3 on v2

--- a/solution.py
+++ b/solution.py
@@ -274,13 +274,17 @@
     return out[0:16, :half] + (out[0:16, half:] + out[16:32, :half])
 
 
-def spread_kernel(recv_ref, values_ref, out_ref):
+def spread_kernel(recv_ref, values_ref, out_ref, near_ref):
     members = recv_ref.shape[0]
     obs = recv_ref[:, COLS:]
     mean = jnp.sum(obs, axis=0, keepdims=True) / members
-    out_ref[0:members, :] = obs - mean
+    pert = obs - mean
+    innovation = values_ref[0:1, :] - mean
+    out_ref[0:members, :] = pert
+    near_ref[0:members, :] = pert
+    near_ref[members:, :] = innovation
     row = lax.broadcasted_iota(jnp.int32, (8, 2 * NOB), 0)
-    out_ref[members:, :] = jnp.where(row == 0, values_ref[...] - mean, 0.0)
+    out_ref[members:, :] = jnp.where(row == 0, innovation, 0.0)
 
 
 def fill_table(table, start, spread_ref):
@@ -362,12 +366,11 @@
     out_ref,
     table,
     res,
-    eye,
+    eyes,
     found,
     full,
     half_s,
     half_u,
-    half_v,
     half_z,
     drives,
 ):
@@ -376,7 +379,8 @@
     fill_table(table, 0, second_ref)
     i0 = lax.broadcasted_iota(jnp.int32, (members, members), 0)
     i1 = lax.broadcasted_iota(jnp.int32, (members, members), 1)
-    eye[...] = jnp.where(i0 == i1, 1.0, 0.0).astype(F32)
+    for n, value in enumerate((scale, 0.84375, 1.5380859375)):
+        eyes[n] = jnp.where(i0 == i1, value, 0.0).astype(F32)
 
     def put(ref, b, x):
         hi, lo = halves(x)
@@ -414,17 +418,15 @@
             norm = jnp.sum(jnp.sum(gram * gram, axis=0, keepdims=True), axis=1, keepdims=True)
             inv = 1.0 / (scale + jnp.sqrt(norm))
             invs.append(inv)
-            s = (scale * eye[...] + gram) * inv
+            s = (eyes[0] + gram) * inv
             full[b] = s
             put(half_s, b, s)
         for b in slots:
             square = product(half_s[b], right_of(half_s, b))
-            s = full[b]
-            put(half_u, b, square)
-            put(half_v, b, 0.0625 * square - 0.5625 * s)
-            full[b] = 2.25 * eye[...] - 2.4375 * s + 1.6875 * square
+            put(half_u, b, 0.25 * square - 1.125 * full[b] + eyes[1])
         for b in slots:
-            put(half_z, b, full[b] + product(half_u[b], right_of(half_v, b)))
+            square = product(half_u[b], right_of(half_u, b))
+            put(half_z, b, square - 0.5390625 * full[b] + eyes[2])
         rows = []
         for b in slots:
             x = jnp.concatenate([dev_ref[pl.ds(base + b, 8, stride=OWNED), :], drives[b]], axis=0)
@@ -549,15 +551,18 @@
     got = lax.all_to_all(
         send.reshape(members, send.shape[2]), "mem", split_axis=0, concat_axis=0, tiled=True
     )
-    spread = call(spread_kernel, sds((SPREAD_ROWS, 2 * NOB)), (got, values))
+    spread, spread_near = call(
+        spread_kernel,
+        [sds((SPREAD_ROWS, 2 * NOB)), sds((members + 1, 2 * NOB))],
+        (got, values),
+    )
     spread_second = lax.ppermute(spread, ("lon", "lat"), off_chip)
-    spread_first = lax.ppermute(spread, "lon", on_chip)
+    spread_first = lax.ppermute(spread_near, "lon", on_chip)
     part, dev, centre = call(
         near_kernel,
         [sds((OWNED, SPREAD_ROWS, LANES)), sds((COLS, members)), sds((COLS, members))],
         (got, near, spread, spread_first),
         [pltpu.VMEM((272, 4 * NOB), BF16)],
-        flops=2 * OWNED * LANES * 272 * 4 * NOB,
     )
     updated = call(
         columns_kernel,
@@ -566,10 +571,10 @@
         [
             pltpu.VMEM((272, 2 * NOB), BF16),
             pltpu.VMEM((COLS, members), F32),
-            pltpu.VMEM((members, members), F32),
+            pltpu.VMEM((3, members, members), F32),
             pltpu.VMEM((BATCH, SPREAD_ROWS, LANES), F32),
             pltpu.VMEM((BATCH, members, members), F32),
-            *[pltpu.VMEM((BATCH, members, 2 * members), BF16)] * 4,
+            *[pltpu.VMEM((BATCH, members, 2 * members), BF16)] * 3,
             pltpu.VMEM((BATCH, 8, members), F32),
         ],
         flops=2 * OWNED * 7 * members * 4 * members * members,

time: 89.4 us -> 89.4 us (level)
  starting transfers between devices: 30.7 us -> 34 us
  waiting for transfers between devices: 15.1 us -> 12.5 us
    ppermute x1, waiting for transfers between devices: 3.74 us -> 0.01 us  [per_device(): spread_second = lax.ppermute(spread, ('lon', 'lat'), off_chip)]
    ppermute x1, starting transfers between devices: 3.58 us -> 6.89 us  [per_device(): spread_first = lax.ppermute(spread_near, 'lon', on_chip)]
    ppermute x1, waiting for transfers between devices: 0.01 us -> 1.16 us  [per_device(): spread_first = lax.ppermute(spread_near, 'lon', on_chip)]
where the time goes in v3:
time: 89.4 us; the launch traced here: 88.8 us
  starting transfers between devices  34 us (38%)
  blocking collectives  25.4 us (28%)
  Pallas kernels  13.8 us (15%)
  waiting for transfers between devices  12.5 us (14%)
  local copies, waits for them, and re-layouts  2.95 us (3%)
    all_to_all x1, blocking collectives, per_device(): lax.all_to_all(send.reshape(members, send.shape[2]), 'mem', split_axis=0,...  15.9 us
    pallas_call x6, Pallas kernels, call(): pl.pallas_call(kernel, out_shape=shapes, in_specs=vmem(len(operands)), ou...  12 us
    ppermute x1, starting transfers between devices, per_device(): other = lax.ppermute(payload, 'lat', [(0, 1), (1, 0)])  10.1 us
    all_to_all x1, blocking collectives, per_device(): lax.all_to_all(updated, 'mem', split_axis=0, concat_axis=0, tiled=True)  9.47 us
    ppermute x1, starting transfers between devices, per_device(): first_in = lax.ppermute(first, 'lon', on_chip)  8.79 us
    ppermute x1, starting transfers between devices, per_device(): spread_first = lax.ppermute(spread_near, 'lon', on_chip)  6.89 us
    ppermute x1, waiting for transfers between devices, per_device(): second_in = lax.ppermute(second, 'lon', off_lon)  5.36 us
    ppermute x1, waiting for transfers between devices, per_device(): corner_in = lax.ppermute(second, ('lon', 'lat'), corners)  4.99 us
  transfers between devices with their start and end apart: 6, of which 4 were waited for; matrix products, arithmetic and copies ran while one was open for 0% of the time, Pallas kernels for 3%

profile of v3, /device:TPU:1, one launch (start us, length us, event | category | flops | bytes accessed | tf_op | source)
XLA Modules:
  0.0 88.8 jit_solution(912625148981279764)
XLA Ops:
  0.0 1.8 %shard_map.82 = (f32[376,128]{1,0:T(8,128)}, f32[16,128]{1,0:T(8,128)}, f32[16,128]{1,0:T(8,128)}, s32[32,128]{1,0:T(8,128)}, f32[32,128]{1,0:T(8,128)}) custom-call(f32[256,128]{1,0:T(8,128)} %bitcast.16, f32[32,128]{1,0:T(8,128)} %bitcast.17, f32[32,128]{1,0:T(8,128)} %bitcast.18, f32[32,128]{1,0:T(8,128)} %bitcast.19, f32[1,256]{1,0:T(1,128)} %bitcast.20, ...), custom_call_target="tpu_custom_call" | custom-call | tf_op jit(solution)/shard_map/pallas_call | solution.py:505
  1.8 8.8 %collective-permute-start = (f32[16,128]{1,0:T(8,128)}, f32[16,128]{1,0:T(8,128)S(1)}, u32[]{:S(2)}, u32[]{:S(2)}) collective-permute-start(f32[16,128]{1,0:T(8,128)} %get-tuple-element.24), channel_id=1, source_target_pairs={{0,2},{2,0},{4,6},{6,4},{8,10},{10,8},{12,14},{14,12},{16,18},{18,... | collective-permute-start | bytes 24584 | tf_op jit(solution)/shard_map/ppermute | solution.py:532
  10.6 1.0 %collective-permute-done.first_ref = f32[16,128]{1,0:T(8,128)S(1)} collective-permute-done((f32[16,128]{1,0:T(8,128)}, f32[16,128]{1,0:T(8,128)S(1)}, u32[]{:S(2)}, u32[]{:S(2)}) %collective-permute-start) | collective-permute-done | bytes 8224 | tf_op jit(solution)/shard_map/ppermute | solution.py:532
  11.6 0.6 constant_dynamic-update-slice_fusion.payload_ref
  12.2 10.1 %collective-permute-start.1 = (f32[376,128]{1,0:T(8,128)}, f32[376,128]{1,0:T(8,128)S(1)}, u32[]{:S(2)}, u32[]{:S(2)}) collective-permute-start(f32[376,128]{1,0:T(8,128)} %constant_dynamic-update-slice_fusion.payload_ref), channel_id=1, source_target_pairs={{0,1},{1,0},{2,3},{3,2},{4,5},{5,4},{6,7},{7,6},{8,9},{9,8},{10,11... | collective-permute-start | bytes 577544 | tf_op jit(solution)/shard_map/ppermute | solution.py:535
  22.3 1.9 %collective-permute-start.2 = (f32[16,128]{1,0:T(8,128)}, f32[16,128]{1,0:T(8,128)S(1)}, u32[]{:S(2)}, u32[]{:S(2)}) collective-permute-start(f32[16,128]{1,0:T(8,128)} %get-tuple-element.32), channel_id=1, source_target_pairs={{0,31},{2,5},{4,3},{6,9},{8,7},{10,13},{12,11},{14,17},{16,15},{18... | collective-permute-start | bytes 24584 | tf_op jit(solution)/shard_map/ppermute | solution.py:542
  24.2 4.5 %collective-permute-start.3 = (f32[16,128]{1,0:T(8,128)}, f32[16,128]{1,0:T(8,128)S(1)}, u32[]{:S(2)}, u32[]{:S(2)}) collective-permute-start(f32[16,128]{1,0:T(8,128)} %get-tuple-element.32), channel_id=1, source_target_pairs={{0,30},{2,4},{4,2},{6,8},{8,6},{10,12},{12,10},{14,16},{16,14},{18... | collective-permute-start | bytes 24584 | tf_op jit(solution)/shard_map/ppermute | solution.py:543
  28.7 0.0 copy-start
  28.7 0.9 %copy-done = f32[376,128]{1,0:T(8,128)S(1)} copy-done((f32[376,128]{1,0:T(8,128)S(1)}, f32[376,128]{1,0:T(8,128)}, u32[]{:S(2)}) %copy-start) | copy-done | bytes 192536
  29.6 0.0 copy-start.1
  29.6 0.7 copy-done.1
  30.3 0.0 copy-start.2
  30.3 0.7 copy-done.2
  31.1 5.0 %collective-permute-done.2.corner_ref = f32[16,128]{1,0:T(8,128)S(1)} collective-permute-done((f32[16,128]{1,0:T(8,128)}, f32[16,128]{1,0:T(8,128)S(1)}, u32[]{:S(2)}, u32[]{:S(2)}) %collective-permute-start.2) | collective-permute-done | bytes 8224 | tf_op jit(solution)/shard_map/ppermute | solution.py:542
  36.1 5.4 %collective-permute-done.3.second_ref = f32[16,128]{1,0:T(8,128)S(1)} collective-permute-done((f32[16,128]{1,0:T(8,128)}, f32[16,128]{1,0:T(8,128)S(1)}, u32[]{:S(2)}, u32[]{:S(2)}) %collective-permute-start.3) | collective-permute-done | bytes 8224 | tf_op jit(solution)/shard_map/ppermute | solution.py:543
  41.4 0.0 collective-permute-done.1.other_ref
  41.4 1.9 %shard_map.84 = (f32[16,8,768]{2,1,0:T(8,128)S(1)}, f32[8,512]{1,0:T(8,128)S(1)}) custom-call(f32[360,128]{1,0:T(8,128)S(1)} %get-tuple-element.31.own_ref, f32[376,128]{1,0:T(8,128)S(1)} %collective-permute-done.1.other_ref, f32[16,128]{1,0:T(8,128)S(1)} %collective-permute-done.2.corner_ref, f32[16,128]{1,0:T(8,128)S(1)} %collective-permute-done.3.second_ref, ...), custom_call_target="tpu_custom_call" | custom-call | tf_op jit(solution)/shard_map/pallas_call | solution.py:471
  43.3 15.9 %all_to_all.17 = f32[16,8,768]{2,1,0:T(8,128)S(1)} all-to-all(f32[16,8,768]{2,1,0:T(8,128)S(1)} %get-tuple-element.33), channel_id=1, replica_groups=mesh['mem'=16,'lon'=16,'lat'=2] {'mem'}, dimensions={0} | all-to-all | bytes 786432 | tf_op jit(solution)/shard_map/all_to_all | solution.py:551
  59.2 0.1 shard_map.85
  59.3 1.9 %collective-permute-start.4 = (f32[136,512]{1,0:T(8,128)S(1)}, f32[136,512]{1,0:T(8,128)S(1)}, u32[]{:S(2)}, u32[]{:S(2)}) collective-permute-start(f32[136,512]{1,0:T(8,128)S(1)} %get-tuple-element.35.mine_ref), channel_id=1, source_target_pairs={{0,31},{2,4},{4,2},{6,8},{8,6},{10,12},{12,10},{14,16},{16,14},{18... | collective-permute-start | bytes 835592 | tf_op jit(solution)/shard_map/ppermute | solution.py:559
  61.2 6.9 %collective-permute-start.5 = (f32[129,512]{1,0:T(8,128)S(1)}, f32[129,512]{1,0:T(8,128)S(1)}, u32[]{:S(2)}, u32[]{:S(2)}) collective-permute-start(f32[129,512]{1,0:T(8,128)S(1)} %get-tuple-element.37), channel_id=1, source_target_pairs={{0,2},{2,0},{4,6},{6,4},{8,10},{10,8},{12,14},{14,12},{16,18},{18,... | collective-permute-start | bytes 792584 | tf_op jit(solution)/shard_map/ppermute | solution.py:560
  68.1 1.2 %collective-permute-done.5.first_ref = f32[129,512]{1,0:T(8,128)S(1)} collective-permute-done((f32[129,512]{1,0:T(8,128)S(1)}, f32[129,512]{1,0:T(8,128)S(1)}, u32[]{:S(2)}, u32[]{:S(2)}) %collective-permute-start.5) | collective-permute-done | bytes 264224 | tf_op jit(solution)/shard_map/ppermute | solution.py:560
  69.3 2.5 %shard_map.86 = (f32[32,136,128]{2,1,0:T(8,128)S(1)}, f32[256,128]{1,0:T(8,128)S(1)}, f32[256,128]{1,0:T(8,128)S(1)}) custom-call(f32[128,768]{1,0:T(8,128)S(1)} %bitcast.12, f32[32,128]{1,0:T(8,128)S(1)} %get-tuple-element.36.places, f32[136,512]{1,0:T(8,128)S(1)} %get-tuple-element.35.mine_ref, f32[129,512]{1,0:T(8,128)S(1)} %collective-permute-done.5.first_ref), custom_call_target="tpu_custom_call" | custom-call | tf_op jit(solution)/shard_map/pallas_call | solution.py:471
  71.8 0.0 collective-permute-done.4.second_ref
  71.8 6.7 %shard_map.87 = f32[128,256]{1,0:T(8,128)S(1)} custom-call(f32[32,128]{1,0:T(8,128)S(1)} %get-tuple-element.29.places, f32[32,128]{1,0:T(8,128)S(1)} %get-tuple-element.30.weight_ref, f32[136,512]{1,0:T(8,128)S(1)} %collective-permute-done.4.second_ref, f32[32,136,128]{2,1,0:T(8,128)S(1)} %get-tuple-element.38.part_ref, ...), custom_call_target="tpu_custom_call" | custom-call | flops 3758096384 | bytes 4194304 | tf_op jit(solution)/shard_map/pallas_call | solution.py:471
  78.5 9.5 %all_to_all.18.recv_ref = f32[16,8,256]{2,1,0:T(8,128)S(1)} all-to-all(f32[16,8,256]{2,1,0:T(8,128)S(1)} %bitcast.13), channel_id=1, replica_groups=mesh['mem'=16,'lon'=16,'lat'=2] {'mem'}, dimensions={0} | all-to-all | bytes 262144 | tf_op jit(solution)/shard_map/all_to_all | solution.py:582
  88.0 0.8 shard_map.88
  (1 shorter events, 0.0 us)
Async XLA Ops:
  1.8 9.8 %collective-permute-start = (f32[16,128]{1,0:T(8,128)}, f32[16,128]{1,0:T(8,128)S(1)}, u32[]{:S(2)}, u32[]{:S(2)}) collective-permute-start(f32[16,128]{1,0:T(8,128)} %get-tuple-element.24), channel_id=1, source_target_pairs={{0,2},{2,0},{4,6},{6,4},{8,10},{10,8},{12,14},{14,12},{16,18},{18,... | collective-permute-start | bytes 24584 | tf_op jit(solution)/shard_map/ppermute | solution.py:532
  12.2 29.2 %collective-permute-start.1 = (f32[376,128]{1,0:T(8,128)}, f32[376,128]{1,0:T(8,128)S(1)}, u32[]{:S(2)}, u32[]{:S(2)}) collective-permute-start(f32[376,128]{1,0:T(8,128)} %constant_dynamic-update-slice_fusion.payload_ref), channel_id=1, source_target_pairs={{0,1},{1,0},{2,3},{3,2},{4,5},{5,4},{6,7},{7,6},{8,9},{9,8},{10,11... | collective-permute-start | bytes 577544 | tf_op jit(solution)/shard_map/ppermute | solution.py:535
  22.3 13.8 %collective-permute-start.2 = (f32[16,128]{1,0:T(8,128)}, f32[16,128]{1,0:T(8,128)S(1)}, u32[]{:S(2)}, u32[]{:S(2)}) collective-permute-start(f32[16,128]{1,0:T(8,128)} %get-tuple-element.32), channel_id=1, source_target_pairs={{0,31},{2,5},{4,3},{6,9},{8,7},{10,13},{12,11},{14,17},{16,15},{18... | collective-permute-start | bytes 24584 | tf_op jit(solution)/shard_map/ppermute | solution.py:542
  24.2 17.2 %collective-permute-start.3 = (f32[16,128]{1,0:T(8,128)}, f32[16,128]{1,0:T(8,128)S(1)}, u32[]{:S(2)}, u32[]{:S(2)}) collective-permute-start(f32[16,128]{1,0:T(8,128)} %get-tuple-element.32), channel_id=1, source_target_pairs={{0,30},{2,4},{4,2},{6,8},{8,6},{10,12},{12,10},{14,16},{16,14},{18... | collective-permute-start | bytes 24584 | tf_op jit(solution)/shard_map/ppermute | solution.py:543
  28.7 0.9 %copy-start = (f32[376,128]{1,0:T(8,128)S(1)}, f32[376,128]{1,0:T(8,128)}, u32[]{:S(2)}) copy-start(f32[376,128]{1,0:T(8,128)} %constant_dynamic-update-slice_fusion.payload_ref) | copy-start | bytes 577540
  29.6 0.7 copy-start.1
  30.3 0.7 copy-start.2
  59.3 12.5 %collective-permute-start.4 = (f32[136,512]{1,0:T(8,128)S(1)}, f32[136,512]{1,0:T(8,128)S(1)}, u32[]{:S(2)}, u32[]{:S(2)}) collective-permute-start(f32[136,512]{1,0:T(8,128)S(1)} %get-tuple-element.35.mine_ref), channel_id=1, source_target_pairs={{0,31},{2,4},{4,2},{6,8},{8,6},{10,12},{12,10},{14,16},{16,14},{18... | collective-permute-start | bytes 835592 | tf_op jit(solution)/shard_map/ppermute | solution.py:559
  61.2 8.1 %collective-permute-start.5 = (f32[129,512]{1,0:T(8,128)S(1)}, f32[129,512]{1,0:T(8,128)S(1)}, u32[]{:S(2)}, u32[]{:S(2)}) collective-permute-start(f32[129,512]{1,0:T(8,128)S(1)} %get-tuple-element.37), channel_id=1, source_target_pairs={{0,2},{2,0},{4,6},{6,4},{8,10},{10,8},{12,14},{14,12},{16,18},{18,... | collective-permute-start | bytes 792584 | tf_op jit(solution)/shard_map/ppermute | solution.py:560

commit v4 on v3

--- a/solution.py
+++ b/solution.py
@@ -19,9 +19,8 @@
 PLANE = LEVELS * ROWS
 VALUE_ROW = 11 * PLANE
 SITE_ROW = VALUE_ROW + 2
-EDGE_ROW = SITE_ROW + 6
+PAYLOAD = SITE_ROW + 6
 EDGE_ROWS = 16
-PAYLOAD = EDGE_ROW + EDGE_ROWS
 COLS = LEVELS * OWNED
 SPREAD_ROWS = 136
 FAR = -8192
@@ -154,7 +153,16 @@
 
 
 def forecast_kernel(
-    own_ref, other_ref, corner_ref, second_ref, first_ref, send_ref, values_ref, coef, state
+    own_ref,
+    other_ref,
+    first_other_ref,
+    second_other_ref,
+    second_ref,
+    first_ref,
+    send_ref,
+    values_ref,
+    coef,
+    state,
 ):
     lane = lane_index()
     here = lat_masks()
@@ -167,9 +175,8 @@
     for block in range(2):
         for tile in range(2):
             part = slice(tile * 8, tile * 8 + 8)
-            far = slice(EDGE_ROW + tile * 8, EDGE_ROW + tile * 8 + 8)
-            a = jnp.where(here[block], first_ref[part, :], other_ref[far, :])
-            b = jnp.where(here[block], second_ref[part, :], corner_ref[part, :])
+            a = jnp.where(here[block], first_ref[part, :], first_other_ref[part, :])
+            b = jnp.where(here[block], second_ref[part, :], second_other_ref[part, :])
             east[block, tile] = jnp.where(even, a, b)
             west[block, tile] = jnp.where(even, b, a)
 
@@ -312,7 +319,7 @@
 
 
 def own_kernel(payload_ref, ids_ref, weight_ref, own_ref, near_ref, far_ref, weight_out):
-    own_ref[...] = payload_ref[0:EDGE_ROW, :]
+    own_ref[...] = payload_ref[...]
     weight_out[...] = weight_ref[...]
     near_ref[...], far_ref[...] = local_places(ids_ref[...])
 
@@ -494,11 +501,12 @@
     lons = lax.axis_size("lon")
     on_chip = [(i, i ^ 1) for i in range(lons)]
     whole = 2 * lons
-    off_chip, corners = [], []
+    off_chip, corners, chip_corners = [], [], []
     for i in range(whole):
         j = (i + 1 if i % 2 else i - 1) % whole
         off_chip.append((i % lons * 2 + i // lons, j % lons * 2 + j // lons))
         corners.append((i % lons * 2 + i // lons, j % lons * 2 + 1 - i // lons))
+        chip_corners.append((i % lons * 2 + i // lons, (i % lons ^ 1) * 2 + 1 - i // lons))
     off_lon = [(i, (i + 1 if i % 2 else i - 1) % lons) for i in range(lons)]
 
     edge = sds((EDGE_ROWS, LANES))
@@ -529,22 +537,21 @@
         neighbours.reshape(ROWS * LANES, LANES),
         loc_weight.reshape(ROWS * LANES, LANES),
     )
+    other = lax.ppermute(payload, "lat", [(0, 1), (1, 0)])
+    first_other = lax.ppermute(first, ("lon", "lat"), chip_corners)
+    second_other = lax.ppermute(second, ("lon", "lat"), corners)
+    second_in = lax.ppermute(second, "lon", off_lon)
     first_in = lax.ppermute(first, "lon", on_chip)
-    payload = lax.dynamic_update_slice(payload, first_in, (EDGE_ROW, 0))
-    payload, second = lax.optimization_barrier((payload, second))
-    other = lax.ppermute(payload, "lat", [(0, 1), (1, 0)])
     own, near, far, weight = call(
         own_kernel,
-        [sds((EDGE_ROW, LANES))] + [sds((OWNED, LANES))] * 3,
+        [sds((PAYLOAD, LANES))] + [sds((OWNED, LANES))] * 3,
         (payload, near_ids, weight),
         flops=1 << 20,
     )
-    corner_in = lax.ppermute(second, ("lon", "lat"), corners)
-    second_in = lax.ppermute(second, "lon", off_lon)
     send, values = call(
         forecast_kernel,
         [sds((mems, MEMBERS_HERE, COLS + 2 * NOB)), sds((8, 2 * NOB))],
-        (own, other, corner_in, second_in, first_in),
+        (own, other, first_other, second_other, second_in, first_in),
         [pltpu.VMEM((8, 5, 2, 8, LANES), F32), pltpu.VMEM((LEVELS, 8, 8, LANES), F32)],
     )
     members = mems * MEMBERS_HERE

time: 89.4 us -> 85.5 us (0.956)
  waiting for transfers between devices: 12.5 us -> 1.41 us
  starting transfers between devices: 34 us -> 42.3 us
    ppermute x1 -> x2, starting transfers between devices: 1.92 us -> 13.8 us  [the longest x1 9.06 us: per_device(): second_other = lax.ppermute(second, ('lon', 'lat'), corners)]
    ppermute x1, starting transfers between devices: 8.79 us -> 1.92 us  [per_device(): first_in = lax.ppermute(first, 'lon', on_chip)]
    ppermute x1, starting transfers between devices: 10.1 us -> 16.3 us  [per_device(): other = lax.ppermute(payload, 'lat', [(0, 1), (1, 0)])]
    ppermute x1, waiting for transfers between devices: 5.36 us -> 0.01 us  [per_device(): second_in = lax.ppermute(second, 'lon', off_lon)]
    ppermute x1 -> x2, waiting for transfers between devices: 4.99 us -> 0.01 us  [the longest x1 0.01 us: per_device(): second_other = lax.ppermute(second, ('lon', 'lat'), corners)]
    ppermute x1, starting transfers between devices: 6.89 us -> 2.05 us  [per_device(): spread_first = lax.ppermute(spread_near, 'lon', on_chip)]
    ppermute x1, starting transfers between devices: 1.92 us -> 4.76 us  [per_device(): spread_second = lax.ppermute(spread, ('lon', 'lat'), off_chip)]
    ppermute x1, waiting for transfers between devices: 1.02 us -> 0.01 us  [per_device(): first_in = lax.ppermute(first, 'lon', on_chip)]
  transfers between devices with their start and end apart: 6 -> 7, of which waited for: 4 -> 1; matrix products, arithmetic and copies ran while one was open for 0% -> 0% of each run, Pallas kernels for 3% -> 3%
where the time goes in v4:
time: 85.5 us; the launch traced here: 84.9 us
  starting transfers between devices  42.3 us (49%)
  blocking collectives  24.8 us (29%)
  Pallas kernels  13.8 us (16%)
  local copies, waits for them, and re-layouts  2.35 us (3%)
  waiting for transfers between devices  1.41 us (2%)
    ppermute x1, starting transfers between devices, per_device(): other = lax.ppermute(payload, 'lat', [(0, 1), (1, 0)])  16.3 us
    all_to_all x1, blocking collectives, per_device(): lax.all_to_all(send.reshape(members, send.shape[2]), 'mem', split_axis=0,...  15.4 us
    pallas_call x6, Pallas kernels, call(): pl.pallas_call(kernel, out_shape=shapes, in_specs=vmem(len(operands)), ou...  12 us
    all_to_all x1, blocking collectives, per_device(): lax.all_to_all(updated, 'mem', split_axis=0, concat_axis=0, tiled=True)  9.47 us
    ppermute x1, starting transfers between devices, per_device(): second_other = lax.ppermute(second, ('lon', 'lat'), corners)  9.06 us
    ppermute x1, starting transfers between devices, per_device(): first_other = lax.ppermute(first, ('lon', 'lat'), chip_corners)  4.77 us
    ppermute x1, starting transfers between devices, per_device(): spread_second = lax.ppermute(spread, ('lon', 'lat'), off_chip)  4.76 us
    ppermute x1, starting transfers between devices, per_device(): second_in = lax.ppermute(second, 'lon', off_lon)  3.48 us
  transfers between devices with their start and end apart: 7, of which 1 were waited for; matrix products, arithmetic and copies ran while one was open for 0% of the time, Pallas kernels for 3%

profile of v4, /device:TPU:1, one launch (start us, length us, event | category | flops | bytes accessed | tf_op | source)
XLA Modules:
  0.0 84.9 jit_solution(6233535702616202197)
XLA Ops:
  0.0 1.8 %shard_map.82 = (f32[360,128]{1,0:T(8,128)}, f32[16,128]{1,0:T(8,128)}, f32[16,128]{1,0:T(8,128)}, s32[32,128]{1,0:T(8,128)}, f32[32,128]{1,0:T(8,128)}) custom-call(f32[256,128]{1,0:T(8,128)} %bitcast.16, f32[32,128]{1,0:T(8,128)} %bitcast.17, f32[32,128]{1,0:T(8,128)} %bitcast.18, f32[32,128]{1,0:T(8,128)} %bitcast.19, f32[1,256]{1,0:T(1,128)} %bitcast.20, ...), custom_call_target="tpu_custom_call" | custom-call | tf_op jit(solution)/shard_map/pallas_call | solution.py:513
  1.8 16.3 %collective-permute-start = (f32[360,128]{1,0:T(8,128)}, f32[360,128]{1,0:T(8,128)S(1)}, u32[]{:S(2)}, u32[]{:S(2)}) collective-permute-start(f32[360,128]{1,0:T(8,128)} %get-tuple-element.21.payload_ref), channel_id=1, source_target_pairs={{0,1},{1,0},{2,3},{3,2},{4,5},{5,4},{6,7},{7,6},{8,9},{9,8},{10,11... | collective-permute-start | bytes 552968 | tf_op jit(solution)/shard_map/ppermute | solution.py:540
  18.1 4.8 %collective-permute-start.1 = (f32[16,128]{1,0:T(8,128)}, f32[16,128]{1,0:T(8,128)S(1)}, u32[]{:S(2)}, u32[]{:S(2)}) collective-permute-start(f32[16,128]{1,0:T(8,128)} %get-tuple-element.27), channel_id=1, source_target_pairs={{0,3},{2,1},{4,7},{6,5},{8,11},{10,9},{12,15},{14,13},{16,19},{18,... | collective-permute-start | bytes 24584 | tf_op jit(solution)/shard_map/ppermute | solution.py:541
  22.8 9.1 %collective-permute-start.2 = (f32[16,128]{1,0:T(8,128)}, f32[16,128]{1,0:T(8,128)S(1)}, u32[]{:S(2)}, u32[]{:S(2)}) collective-permute-start(f32[16,128]{1,0:T(8,128)} %get-tuple-element.28), channel_id=1, source_target_pairs={{0,31},{2,5},{4,3},{6,9},{8,7},{10,13},{12,11},{14,17},{16,15},{18... | collective-permute-start | bytes 24584 | tf_op jit(solution)/shard_map/ppermute | solution.py:542
  31.9 3.5 %collective-permute-start.3 = (f32[16,128]{1,0:T(8,128)}, f32[16,128]{1,0:T(8,128)S(1)}, u32[]{:S(2)}, u32[]{:S(2)}) collective-permute-start(f32[16,128]{1,0:T(8,128)} %get-tuple-element.28), channel_id=1, source_target_pairs={{0,30},{2,4},{4,2},{6,8},{8,6},{10,12},{12,10},{14,16},{16,14},{18... | collective-permute-start | bytes 24584 | tf_op jit(solution)/shard_map/ppermute | solution.py:543
  35.4 1.9 %collective-permute-start.4 = (f32[16,128]{1,0:T(8,128)}, f32[16,128]{1,0:T(8,128)S(1)}, u32[]{:S(2)}, u32[]{:S(2)}) collective-permute-start(f32[16,128]{1,0:T(8,128)} %get-tuple-element.27), channel_id=1, source_target_pairs={{0,2},{2,0},{4,6},{6,4},{8,10},{10,8},{12,14},{14,12},{16,18},{18,... | collective-permute-start | bytes 24584 | tf_op jit(solution)/shard_map/ppermute | solution.py:544
  37.3 0.0 copy-start
  37.3 0.9 %copy-done = f32[360,128]{1,0:T(8,128)S(1)} copy-done((f32[360,128]{1,0:T(8,128)S(1)}, f32[360,128]{1,0:T(8,128)}, u32[]{:S(2)}) %copy-start) | copy-done | bytes 184344
  38.2 0.0 copy-start.1
  38.2 0.7 copy-done.1
  39.0 0.0 copy-start.2
  39.0 0.7 copy-done.2
  39.7 0.0 collective-permute-done.1.first_other_ref
  39.7 0.0 collective-permute-done.2.second_other_ref
  39.7 0.0 collective-permute-done.3.second_ref
  39.7 0.0 collective-permute-done.4.first_ref
  39.7 0.0 collective-permute-done.other_ref
  39.8 1.9 %shard_map.84 = (f32[16,8,768]{2,1,0:T(8,128)S(1)}, f32[8,512]{1,0:T(8,128)S(1)}) custom-call(f32[360,128]{1,0:T(8,128)S(1)} %get-tuple-element.26.own_ref, f32[360,128]{1,0:T(8,128)S(1)} %collective-permute-done.other_ref, f32[16,128]{1,0:T(8,128)S(1)} %collective-permute-done.1.first_other_ref, f32[16,128]{1,0:T(8,128)S(1)} %collective-permute-done.2.second_other_ref, ...), custom_call_target="tpu_custom_call" | custom-call | tf_op jit(solution)/shard_map/pallas_call | solution.py:478
  41.6 15.4 %all_to_all.17 = f32[16,8,768]{2,1,0:T(8,128)S(1)} all-to-all(f32[16,8,768]{2,1,0:T(8,128)S(1)} %get-tuple-element.29), channel_id=1, replica_groups=mesh['mem'=16,'lon'=16,'lat'=2] {'mem'}, dimensions={0} | all-to-all | bytes 786432 | tf_op jit(solution)/shard_map/all_to_all | solution.py:558
  57.0 0.1 shard_map.85
  57.1 4.8 %collective-permute-start.5 = (f32[136,512]{1,0:T(8,128)S(1)}, f32[136,512]{1,0:T(8,128)S(1)}, u32[]{:S(2)}, u32[]{:S(2)}) collective-permute-start(f32[136,512]{1,0:T(8,128)S(1)} %get-tuple-element.31.mine_ref), channel_id=1, source_target_pairs={{0,31},{2,4},{4,2},{6,8},{8,6},{10,12},{12,10},{14,16},{16,14},{18... | collective-permute-start | bytes 835592 | tf_op jit(solution)/shard_map/ppermute | solution.py:566
  61.9 2.1 %collective-permute-start.6 = (f32[129,512]{1,0:T(8,128)S(1)}, f32[129,512]{1,0:T(8,128)S(1)}, u32[]{:S(2)}, u32[]{:S(2)}) collective-permute-start(f32[129,512]{1,0:T(8,128)S(1)} %get-tuple-element.33), channel_id=1, source_target_pairs={{0,2},{2,0},{4,6},{6,4},{8,10},{10,8},{12,14},{14,12},{16,18},{18,... | collective-permute-start | bytes 792584 | tf_op jit(solution)/shard_map/ppermute | solution.py:567
  63.9 1.4 %collective-permute-done.6.first_ref = f32[129,512]{1,0:T(8,128)S(1)} collective-permute-done((f32[129,512]{1,0:T(8,128)S(1)}, f32[129,512]{1,0:T(8,128)S(1)}, u32[]{:S(2)}, u32[]{:S(2)}) %collective-permute-start.6) | collective-permute-done | bytes 264224 | tf_op jit(solution)/shard_map/ppermute | solution.py:567
  65.3 2.5 %shard_map.86 = (f32[32,136,128]{2,1,0:T(8,128)S(1)}, f32[256,128]{1,0:T(8,128)S(1)}, f32[256,128]{1,0:T(8,128)S(1)}) custom-call(f32[128,768]{1,0:T(8,128)S(1)} %bitcast.12, f32[32,128]{1,0:T(8,128)S(1)} %get-tuple-element.32.places, f32[136,512]{1,0:T(8,128)S(1)} %get-tuple-element.31.mine_ref, f32[129,512]{1,0:T(8,128)S(1)} %collective-permute-done.6.first_ref), custom_call_target="tpu_custom_call" | custom-call | tf_op jit(solution)/shard_map/pallas_call | solution.py:478
  67.8 0.0 collective-permute-done.5.second_ref
  67.8 6.7 %shard_map.87 = f32[128,256]{1,0:T(8,128)S(1)} custom-call(f32[32,128]{1,0:T(8,128)S(1)} %get-tuple-element.24.places, f32[32,128]{1,0:T(8,128)S(1)} %get-tuple-element.25.weight_ref, f32[136,512]{1,0:T(8,128)S(1)} %collective-permute-done.5.second_ref, f32[32,136,128]{2,1,0:T(8,128)S(1)} %get-tuple-element.34.part_ref, ...), custom_call_target="tpu_custom_call" | custom-call | flops 3758096384 | bytes 4194304 | tf_op jit(solution)/shard_map/pallas_call | solution.py:478
  74.5 9.5 %all_to_all.18.recv_ref = f32[16,8,256]{2,1,0:T(8,128)S(1)} all-to-all(f32[16,8,256]{2,1,0:T(8,128)S(1)} %bitcast.13), channel_id=1, replica_groups=mesh['mem'=16,'lon'=16,'lat'=2] {'mem'}, dimensions={0} | all-to-all | bytes 262144 | tf_op jit(solution)/shard_map/all_to_all | solution.py:589
  84.0 0.8 shard_map.88
  (1 shorter events, 0.0 us)
Async XLA Ops:
  1.8 38.0 %collective-permute-start = (f32[360,128]{1,0:T(8,128)}, f32[360,128]{1,0:T(8,128)S(1)}, u32[]{:S(2)}, u32[]{:S(2)}) collective-permute-start(f32[360,128]{1,0:T(8,128)} %get-tuple-element.21.payload_ref), channel_id=1, source_target_pairs={{0,1},{1,0},{2,3},{3,2},{4,5},{5,4},{6,7},{7,6},{8,9},{9,8},{10,11... | collective-permute-start | bytes 552968 | tf_op jit(solution)/shard_map/ppermute | solution.py:540
  18.1 21.7 %collective-permute-start.1 = (f32[16,128]{1,0:T(8,128)}, f32[16,128]{1,0:T(8,128)S(1)}, u32[]{:S(2)}, u32[]{:S(2)}) collective-permute-start(f32[16,128]{1,0:T(8,128)} %get-tuple-element.27), channel_id=1, source_target_pairs={{0,3},{2,1},{4,7},{6,5},{8,11},{10,9},{12,15},{14,13},{16,19},{18,... | collective-permute-start | bytes 24584 | tf_op jit(solution)/shard_map/ppermute | solution.py:541
  22.8 16.9 %collective-permute-start.2 = (f32[16,128]{1,0:T(8,128)}, f32[16,128]{1,0:T(8,128)S(1)}, u32[]{:S(2)}, u32[]{:S(2)}) collective-permute-start(f32[16,128]{1,0:T(8,128)} %get-tuple-element.28), channel_id=1, source_target_pairs={{0,31},{2,5},{4,3},{6,9},{8,7},{10,13},{12,11},{14,17},{16,15},{18... | collective-permute-start | bytes 24584 | tf_op jit(solution)/shard_map/ppermute | solution.py:542
  31.9 7.8 %collective-permute-start.3 = (f32[16,128]{1,0:T(8,128)}, f32[16,128]{1,0:T(8,128)S(1)}, u32[]{:S(2)}, u32[]{:S(2)}) collective-permute-start(f32[16,128]{1,0:T(8,128)} %get-tuple-element.28), channel_id=1, source_target_pairs={{0,30},{2,4},{4,2},{6,8},{8,6},{10,12},{12,10},{14,16},{16,14},{18... | collective-permute-start | bytes 24584 | tf_op jit(solution)/shard_map/ppermute | solution.py:543
  35.4 4.4 %collective-permute-start.4 = (f32[16,128]{1,0:T(8,128)}, f32[16,128]{1,0:T(8,128)S(1)}, u32[]{:S(2)}, u32[]{:S(2)}) collective-permute-start(f32[16,128]{1,0:T(8,128)} %get-tuple-element.27), channel_id=1, source_target_pairs={{0,2},{2,0},{4,6},{6,4},{8,10},{10,8},{12,14},{14,12},{16,18},{18,... | collective-permute-start | bytes 24584 | tf_op jit(solution)/shard_map/ppermute | solution.py:544
  37.3 0.9 %copy-start = (f32[360,128]{1,0:T(8,128)S(1)}, f32[360,128]{1,0:T(8,128)}, u32[]{:S(2)}) copy-start(f32[360,128]{1,0:T(8,128)} %get-tuple-element.21.payload_ref) | copy-start | bytes 552964
  38.2 0.7 copy-start.1
  39.0 0.7 copy-start.2
  57.1 10.7 %collective-permute-start.5 = (f32[136,512]{1,0:T(8,128)S(1)}, f32[136,512]{1,0:T(8,128)S(1)}, u32[]{:S(2)}, u32[]{:S(2)}) collective-permute-start(f32[136,512]{1,0:T(8,128)S(1)} %get-tuple-element.31.mine_ref), channel_id=1, source_target_pairs={{0,31},{2,4},{4,2},{6,8},{8,6},{10,12},{12,10},{14,16},{16,14},{18... | collective-permute-start | bytes 835592 | tf_op jit(solution)/shard_map/ppermute | solution.py:566
  61.9 3.5 %collective-permute-start.6 = (f32[129,512]{1,0:T(8,128)S(1)}, f32[129,512]{1,0:T(8,128)S(1)}, u32[]{:S(2)}, u32[]{:S(2)}) collective-permute-start(f32[129,512]{1,0:T(8,128)S(1)} %get-tuple-element.33), channel_id=1, source_target_pairs={{0,2},{2,0},{4,6},{6,4},{8,10},{10,8},{12,14},{14,12},{16,18},{18,... | collective-permute-start | bytes 792584 | tf_op jit(solution)/shard_map/ppermute | solution.py:567

commit v5 on v4

--- a/solution.py
+++ b/solution.py
@@ -156,8 +156,8 @@
     own_ref,
     other_ref,
     first_other_ref,
+    second_ref,
     second_other_ref,
-    second_ref,
     first_ref,
     send_ref,
     values_ref,
@@ -318,10 +318,8 @@
     return near.astype(F32), far.astype(F32)
 
 
-def own_kernel(payload_ref, ids_ref, weight_ref, own_ref, near_ref, far_ref, weight_out):
+def own_kernel(payload_ref, own_ref):
     own_ref[...] = payload_ref[...]
-    weight_out[...] = weight_ref[...]
-    near_ref[...], far_ref[...] = local_places(ids_ref[...])
 
 
 def gather_pair(table, places, first_column, blocks):
@@ -342,11 +340,12 @@
 
 
 def near_kernel(
-    recv_ref, places, mine_ref, first_ref, part_ref, dev_ref, centre_ref, table
+    recv_ref, ids_ref, mine_ref, first_ref, part_ref, dev_ref, centre_ref, table, places
 ):
     members = recv_ref.shape[0]
     fill_table(table, 0, mine_ref)
     fill_table(table, 2 * NOB, first_ref)
+    places[...] = local_places(ids_ref[...])[0]
     traces = jnp.transpose(recv_ref[:, :COLS])
     centre = jnp.sum(traces, axis=1, keepdims=True) / members
     dev_ref[...] = traces - centre
@@ -364,7 +363,7 @@
 
 
 def columns_kernel(
-    places,
+    ids_ref,
     weight_ref,
     second_ref,
     part_ref,
@@ -372,6 +371,7 @@
     centre_ref,
     out_ref,
     table,
+    places,
     res,
     eyes,
     found,
@@ -384,6 +384,7 @@
     members = 128
     scale = members - 1.0
     fill_table(table, 0, second_ref)
+    places[...] = local_places(ids_ref[...])[1]
     i0 = lax.broadcasted_iota(jnp.int32, (members, members), 0)
     i1 = lax.broadcasted_iota(jnp.int32, (members, members), 1)
     for n, value in enumerate((scale, 0.84375, 1.5380859375)):
@@ -539,19 +540,14 @@
     )
     other = lax.ppermute(payload, "lat", [(0, 1), (1, 0)])
     first_other = lax.ppermute(first, ("lon", "lat"), chip_corners)
+    second_in = lax.ppermute(second, "lon", off_lon)
     second_other = lax.ppermute(second, ("lon", "lat"), corners)
-    second_in = lax.ppermute(second, "lon", off_lon)
     first_in = lax.ppermute(first, "lon", on_chip)
-    own, near, far, weight = call(
-        own_kernel,
-        [sds((PAYLOAD, LANES))] + [sds((OWNED, LANES))] * 3,
-        (payload, near_ids, weight),
-        flops=1 << 20,
-    )
+    own = call(own_kernel, sds((PAYLOAD, LANES)), (payload,), flops=1 << 20)
     send, values = call(
         forecast_kernel,
         [sds((mems, MEMBERS_HERE, COLS + 2 * NOB)), sds((8, 2 * NOB))],
-        (own, other, first_other, second_other, second_in, first_in),
+        (own, other, first_other, second_in, second_other, first_in),
         [pltpu.VMEM((8, 5, 2, 8, LANES), F32), pltpu.VMEM((LEVELS, 8, 8, LANES), F32)],
     )
     members = mems * MEMBERS_HERE
@@ -568,15 +564,16 @@
     part, dev, centre = call(
         near_kernel,
         [sds((OWNED, SPREAD_ROWS, LANES)), sds((COLS, members)), sds((COLS, members))],
-        (got, near, spread, spread_first),
-        [pltpu.VMEM((272, 4 * NOB), BF16)],
+        (got, near_ids, spread, spread_first),
+        [pltpu.VMEM((272, 4 * NOB), BF16), pltpu.VMEM((OWNED, LANES), F32)],
     )
     updated = call(
         columns_kernel,
         sds((members, COLS)),
-        (far, weight, spread_second, part, dev, centre),
+        (near_ids, weight, spread_second, part, dev, centre),
         [
             pltpu.VMEM((272, 2 * NOB), BF16),
+            pltpu.VMEM((OWNED, LANES), F32),
             pltpu.VMEM((COLS, members), F32),
             pltpu.VMEM((3, members, members), F32),
             pltpu.VMEM((BATCH, SPREAD_ROWS, LANES), F32),

time: 85.5 us -> 86.8 us (1.015)
  blocking collectives: 24.8 us -> 27.5 us
  starting transfers between devices: 42.3 us -> 41.4 us
    ppermute x1, starting transfers between devices: 4.76 us -> 2.16 us  [per_device(): spread_second = lax.ppermute(spread, ('lon', 'lat'), off_chip)]
    all_to_all x1, blocking collectives: 15.4 us -> 17.7 us  [per_device(): lax.all_to_all(send.reshape(members, send.shape[2]), 'mem', split_axis=0,...]
    ppermute x1, starting transfers between devices: 2.05 us -> 3.79 us  [per_device(): spread_first = lax.ppermute(spread_near, 'lon', on_chip)]
    ppermute x1, starting transfers between devices: 3.48 us -> 1.92 us  [per_device(): second_in = lax.ppermute(second, 'lon', off_lon)]
    ppermute x1, starting transfers between devices: 9.06 us -> 10.6 us  [per_device(): second_other = lax.ppermute(second, ('lon', 'lat'), corners)]
  transfers between devices with their start and end apart: 7 -> 7, of which waited for: 1 -> 2; matrix products, arithmetic and copies ran while one was open for 0% -> 0% of each run, Pallas kernels for 3% -> 3%
where the time goes in v5:
time: 86.8 us; the launch traced here: 86.3 us
  starting transfers between devices  41.4 us (48%)
  blocking collectives  27.5 us (32%)
  Pallas kernels  13.8 us (16%)
  waiting for transfers between devices  1.77 us (2%)
  local copies, waits for them, and re-layouts  1.64 us (2%)
    all_to_all x1, blocking collectives, per_device(): lax.all_to_all(send.reshape(members, send.shape[2]), 'mem', split_axis=0,...  17.7 us
    ppermute x1, starting transfers between devices, per_device(): other = lax.ppermute(payload, 'lat', [(0, 1), (1, 0)])  16.3 us
    pallas_call x6, Pallas kernels, call(): pl.pallas_call(kernel, out_shape=shapes, in_specs=vmem(len(operands)), ou...  12.1 us
    ppermute x1, starting transfers between devices, per_device(): second_other = lax.ppermute(second, ('lon', 'lat'), corners)  10.6 us
    all_to_all x1, blocking collectives, per_device(): lax.all_to_all(updated, 'mem', split_axis=0, concat_axis=0, tiled=True)  9.72 us
    ppermute x1, starting transfers between devices, per_device(): first_other = lax.ppermute(first, ('lon', 'lat'), chip_corners)  4.77 us
    ppermute x1, starting transfers between devices, per_device(): spread_first = lax.ppermute(spread_near, 'lon', on_chip)  3.79 us
    ppermute x1, starting transfers between devices, per_device(): spread_second = lax.ppermute(spread, ('lon', 'lat'), off_chip)  2.16 us
  transfers between devices with their start and end apart: 7, of which 2 were waited for; matrix products, arithmetic and copies ran while one was open for 0% of the time, Pallas kernels for 3%

profile of v5, /device:TPU:1, one launch (start us, length us, event | category | flops | bytes accessed | tf_op | source)
XLA Modules:
  0.0 86.3 jit_solution(15321562808694798148)
XLA Ops:
  0.0 1.8 %shard_map.82 = (f32[360,128]{1,0:T(8,128)}, f32[16,128]{1,0:T(8,128)}, f32[16,128]{1,0:T(8,128)}, s32[32,128]{1,0:T(8,128)}, f32[32,128]{1,0:T(8,128)}) custom-call(f32[256,128]{1,0:T(8,128)} %bitcast.16, f32[32,128]{1,0:T(8,128)} %bitcast.17, f32[32,128]{1,0:T(8,128)} %bitcast.18, f32[32,128]{1,0:T(8,128)} %bitcast.19, f32[1,256]{1,0:T(1,128)} %bitcast.20, ...), custom_call_target="tpu_custom_call" | custom-call | tf_op jit(solution)/shard_map/pallas_call | solution.py:514
  1.8 16.3 %collective-permute-start = (f32[360,128]{1,0:T(8,128)}, f32[360,128]{1,0:T(8,128)S(1)}, u32[]{:S(2)}, u32[]{:S(2)}) collective-permute-start(f32[360,128]{1,0:T(8,128)} %get-tuple-element.19.payload_ref), channel_id=1, source_target_pairs={{0,1},{1,0},{2,3},{3,2},{4,5},{5,4},{6,7},{7,6},{8,9},{9,8},{10,11... | collective-permute-start | bytes 552968 | tf_op jit(solution)/shard_map/ppermute | solution.py:541
  18.1 4.8 %collective-permute-start.1 = (f32[16,128]{1,0:T(8,128)}, f32[16,128]{1,0:T(8,128)S(1)}, u32[]{:S(2)}, u32[]{:S(2)}) collective-permute-start(f32[16,128]{1,0:T(8,128)} %get-tuple-element.20), channel_id=1, source_target_pairs={{0,3},{2,1},{4,7},{6,5},{8,11},{10,9},{12,15},{14,13},{16,19},{18,... | collective-permute-start | bytes 24584 | tf_op jit(solution)/shard_map/ppermute | solution.py:542
  22.8 1.9 %collective-permute-start.2 = (f32[16,128]{1,0:T(8,128)}, f32[16,128]{1,0:T(8,128)S(1)}, u32[]{:S(2)}, u32[]{:S(2)}) collective-permute-start(f32[16,128]{1,0:T(8,128)} %get-tuple-element.21), channel_id=1, source_target_pairs={{0,30},{2,4},{4,2},{6,8},{8,6},{10,12},{12,10},{14,16},{16,14},{18... | collective-permute-start | bytes 24584 | tf_op jit(solution)/shard_map/ppermute | solution.py:543
  24.8 10.6 %collective-permute-start.3 = (f32[16,128]{1,0:T(8,128)}, f32[16,128]{1,0:T(8,128)S(1)}, u32[]{:S(2)}, u32[]{:S(2)}) collective-permute-start(f32[16,128]{1,0:T(8,128)} %get-tuple-element.21), channel_id=1, source_target_pairs={{0,31},{2,5},{4,3},{6,9},{8,7},{10,13},{12,11},{14,17},{16,15},{18... | collective-permute-start | bytes 24584 | tf_op jit(solution)/shard_map/ppermute | solution.py:544
  35.4 1.9 %collective-permute-start.4 = (f32[16,128]{1,0:T(8,128)}, f32[16,128]{1,0:T(8,128)S(1)}, u32[]{:S(2)}, u32[]{:S(2)}) collective-permute-start(f32[16,128]{1,0:T(8,128)} %get-tuple-element.20), channel_id=1, source_target_pairs={{0,2},{2,0},{4,6},{6,4},{8,10},{10,8},{12,14},{14,12},{16,18},{18,... | collective-permute-start | bytes 24584 | tf_op jit(solution)/shard_map/ppermute | solution.py:545
  37.3 0.0 copy-start
  37.3 0.9 %copy-done = f32[360,128]{1,0:T(8,128)S(1)} copy-done((f32[360,128]{1,0:T(8,128)S(1)}, f32[360,128]{1,0:T(8,128)}, u32[]{:S(2)}) %copy-start) | copy-done | bytes 184344
  38.2 0.0 copy-start.2
  38.3 0.0 collective-permute-done.1.first_other_ref
  38.3 0.0 collective-permute-done.2.second_ref
  38.3 0.6 collective-permute-done.3.second_other_ref
  38.9 0.0 collective-permute-done.4.first_ref
  38.9 0.0 collective-permute-done.other_ref
  38.9 1.9 %shard_map.84 = (f32[16,8,768]{2,1,0:T(8,128)S(1)}, f32[8,512]{1,0:T(8,128)S(1)}) custom-call(f32[360,128]{1,0:T(8,128)S(1)} %shard_map.83.own_ref, f32[360,128]{1,0:T(8,128)S(1)} %collective-permute-done.other_ref, f32[16,128]{1,0:T(8,128)S(1)} %collective-permute-done.1.first_other_ref, f32[16,128]{1,0:T(8,128)S(1)} %collective-permute-done.2.second_ref, ...), custom_call_target="tpu_custom_call" | custom-call | tf_op jit(solution)/shard_map/pallas_call | solution.py:479
  40.8 17.7 %all_to_all.17 = f32[16,8,768]{2,1,0:T(8,128)S(1)} all-to-all(f32[16,8,768]{2,1,0:T(8,128)S(1)} %get-tuple-element.22), channel_id=1, replica_groups=mesh['mem'=16,'lon'=16,'lat'=2] {'mem'}, dimensions={0} | all-to-all | bytes 786432 | tf_op jit(solution)/shard_map/all_to_all | solution.py:554
  58.5 0.1 shard_map.85
  58.6 2.2 %collective-permute-start.5 = (f32[136,512]{1,0:T(8,128)S(1)}, f32[136,512]{1,0:T(8,128)S(1)}, u32[]{:S(2)}, u32[]{:S(2)}) collective-permute-start(f32[136,512]{1,0:T(8,128)S(1)} %get-tuple-element.24.mine_ref), channel_id=1, source_target_pairs={{0,31},{2,4},{4,2},{6,8},{8,6},{10,12},{12,10},{14,16},{16,14},{18... | collective-permute-start | bytes 835592 | tf_op jit(solution)/shard_map/ppermute | solution.py:562
  60.8 3.8 %collective-permute-start.6 = (f32[129,512]{1,0:T(8,128)S(1)}, f32[129,512]{1,0:T(8,128)S(1)}, u32[]{:S(2)}, u32[]{:S(2)}) collective-permute-start(f32[129,512]{1,0:T(8,128)S(1)} %get-tuple-element.25), channel_id=1, source_target_pairs={{0,2},{2,0},{4,6},{6,4},{8,10},{10,8},{12,14},{14,12},{16,18},{18,... | collective-permute-start | bytes 792584 | tf_op jit(solution)/shard_map/ppermute | solution.py:563
  64.6 1.2 %collective-permute-done.6.first_ref = f32[129,512]{1,0:T(8,128)S(1)} collective-permute-done((f32[129,512]{1,0:T(8,128)S(1)}, f32[129,512]{1,0:T(8,128)S(1)}, u32[]{:S(2)}, u32[]{:S(2)}) %collective-permute-start.6) | collective-permute-done | bytes 264224 | tf_op jit(solution)/shard_map/ppermute | solution.py:563
  65.7 0.0 copy-start.1
  65.7 0.7 copy-done.1
  66.4 2.5 %shard_map.86 = (f32[32,136,128]{2,1,0:T(8,128)S(1)}, f32[256,128]{1,0:T(8,128)S(1)}, f32[256,128]{1,0:T(8,128)S(1)}) custom-call(f32[128,768]{1,0:T(8,128)S(1)} %bitcast.12, s32[32,128]{1,0:T(8,128)S(1)} %copy-done.1, f32[136,512]{1,0:T(8,128)S(1)} %get-tuple-element.24.mine_ref, f32[129,512]{1,0:T(8,128)S(1)} %collective-permute-done.6.first_ref), custom_call_target="tpu_custom_call" | custom-call | tf_op jit(solution)/shard_map/pallas_call | solution.py:479
  68.9 0.0 collective-permute-done.5.second_ref
  68.9 0.0 copy-done.2
  69.0 6.8 %shard_map.87 = f32[128,256]{1,0:T(8,128)S(1)} custom-call(s32[32,128]{1,0:T(8,128)S(1)} %copy-done.1, f32[32,128]{1,0:T(8,128)S(1)} %copy-done.2, f32[136,512]{1,0:T(8,128)S(1)} %collective-permute-done.5.second_ref, f32[32,136,128]{2,1,0:T(8,128)S(1)} %get-tuple-element.26.part_ref, f32[256,128]{1,0:T(8,128)S(1)} %get-tuple-element.27.dev_ref, ...), custom_call_target="tpu_custom_call" | custom-call | flops 3758096384 | bytes 4194304 | tf_op jit(solution)/shard_map/pallas_call | solution.py:479
  75.7 9.7 %all_to_all.18.recv_ref = f32[16,8,256]{2,1,0:T(8,128)S(1)} all-to-all(f32[16,8,256]{2,1,0:T(8,128)S(1)} %bitcast.13), channel_id=1, replica_groups=mesh['mem'=16,'lon'=16,'lat'=2] {'mem'}, dimensions={0} | all-to-all | bytes 262144 | tf_op jit(solution)/shard_map/all_to_all | solution.py:586
  85.5 0.8 shard_map.88
  (1 shorter events, 0.0 us)
Async XLA Ops:
  1.8 37.1 %collective-permute-start = (f32[360,128]{1,0:T(8,128)}, f32[360,128]{1,0:T(8,128)S(1)}, u32[]{:S(2)}, u32[]{:S(2)}) collective-permute-start(f32[360,128]{1,0:T(8,128)} %get-tuple-element.19.payload_ref), channel_id=1, source_target_pairs={{0,1},{1,0},{2,3},{3,2},{4,5},{5,4},{6,7},{7,6},{8,9},{9,8},{10,11... | collective-permute-start | bytes 552968 | tf_op jit(solution)/shard_map/ppermute | solution.py:541
  18.1 20.2 %collective-permute-start.1 = (f32[16,128]{1,0:T(8,128)}, f32[16,128]{1,0:T(8,128)S(1)}, u32[]{:S(2)}, u32[]{:S(2)}) collective-permute-start(f32[16,128]{1,0:T(8,128)} %get-tuple-element.20), channel_id=1, source_target_pairs={{0,3},{2,1},{4,7},{6,5},{8,11},{10,9},{12,15},{14,13},{16,19},{18,... | collective-permute-start | bytes 24584 | tf_op jit(solution)/shard_map/ppermute | solution.py:542
  22.8 15.4 %collective-permute-start.2 = (f32[16,128]{1,0:T(8,128)}, f32[16,128]{1,0:T(8,128)S(1)}, u32[]{:S(2)}, u32[]{:S(2)}) collective-permute-start(f32[16,128]{1,0:T(8,128)} %get-tuple-element.21), channel_id=1, source_target_pairs={{0,30},{2,4},{4,2},{6,8},{8,6},{10,12},{12,10},{14,16},{16,14},{18... | collective-permute-start | bytes 24584 | tf_op jit(solution)/shard_map/ppermute | solution.py:543
  24.8 14.1 %collective-permute-start.3 = (f32[16,128]{1,0:T(8,128)}, f32[16,128]{1,0:T(8,128)S(1)}, u32[]{:S(2)}, u32[]{:S(2)}) collective-permute-start(f32[16,128]{1,0:T(8,128)} %get-tuple-element.21), channel_id=1, source_target_pairs={{0,31},{2,5},{4,3},{6,9},{8,7},{10,13},{12,11},{14,17},{16,15},{18... | collective-permute-start | bytes 24584 | tf_op jit(solution)/shard_map/ppermute | solution.py:544
  35.4 3.5 %collective-permute-start.4 = (f32[16,128]{1,0:T(8,128)}, f32[16,128]{1,0:T(8,128)S(1)}, u32[]{:S(2)}, u32[]{:S(2)}) collective-permute-start(f32[16,128]{1,0:T(8,128)} %get-tuple-element.20), channel_id=1, source_target_pairs={{0,2},{2,0},{4,6},{6,4},{8,10},{10,8},{12,14},{14,12},{16,18},{18,... | collective-permute-start | bytes 24584 | tf_op jit(solution)/shard_map/ppermute | solution.py:545
  37.3 0.9 %copy-start = (f32[360,128]{1,0:T(8,128)S(1)}, f32[360,128]{1,0:T(8,128)}, u32[]{:S(2)}) copy-start(f32[360,128]{1,0:T(8,128)} %get-tuple-element.19.payload_ref) | copy-start | bytes 552964
  38.2 30.7 %copy-start.2 = (f32[32,128]{1,0:T(8,128)S(1)}, f32[32,128]{1,0:T(8,128)}, u32[]{:S(2)}) copy-start(f32[32,128]{1,0:T(8,128)} %get-tuple-element.18.weight_ref) | copy-start | bytes 49156
  58.6 10.4 %collective-permute-start.5 = (f32[136,512]{1,0:T(8,128)S(1)}, f32[136,512]{1,0:T(8,128)S(1)}, u32[]{:S(2)}, u32[]{:S(2)}) collective-permute-start(f32[136,512]{1,0:T(8,128)S(1)} %get-tuple-element.24.mine_ref), channel_id=1, source_target_pairs={{0,31},{2,4},{4,2},{6,8},{8,6},{10,12},{12,10},{14,16},{16,14},{18... | collective-permute-start | bytes 835592 | tf_op jit(solution)/shard_map/ppermute | solution.py:562
  60.8 5.0 %collective-permute-start.6 = (f32[129,512]{1,0:T(8,128)S(1)}, f32[129,512]{1,0:T(8,128)S(1)}, u32[]{:S(2)}, u32[]{:S(2)}) collective-permute-start(f32[129,512]{1,0:T(8,128)S(1)} %get-tuple-element.25), channel_id=1, source_target_pairs={{0,2},{2,0},{4,6},{6,4},{8,10},{10,8},{12,14},{14,12},{16,18},{18,... | collective-permute-start | bytes 792584 | tf_op jit(solution)/shard_map/ppermute | solution.py:563
  65.7 0.7 copy-start.1

commit v6 on v4

--- a/solution.py
+++ b/solution.py
@@ -86,10 +86,10 @@
     out_ref,
     first_ref,
     second_ref,
-    ids_out,
-    weight_out,
+    extra_ref,
     value,
     site,
+    ids,
     sems,
 ):
     owned = pl.ds(pl.multiple_of(lax.axis_index("mem") * OWNED, OWNED), OWNED)
@@ -101,14 +101,15 @@
         ],
         (value_ref, value),
         (site_ref, site),
-        (ids_ref.at[owned, :], ids_out),
-        (weight_ref.at[owned, :], weight_out),
+        (ids_ref.at[owned, :], ids),
+        (weight_ref.at[owned, :], extra_ref.at[pl.ds(OWNED, OWNED), :]),
     ]
     copies = [pltpu.make_async_copy(src, dst, sems.at[n]) for n, (src, dst) in enumerate(moves)]
     for copy in copies:
         copy.start()
     for copy in copies:
         copy.wait()
+    extra_ref[0:OWNED, :] = ids[...].astype(F32)
     values = value[...]
     sites = site[...].astype(F32)
     rest = jnp.zeros((PAYLOAD - SITE_ROW - 2, LANES), F32)
@@ -318,10 +319,10 @@
     return near.astype(F32), far.astype(F32)
 
 
-def own_kernel(payload_ref, ids_ref, weight_ref, own_ref, near_ref, far_ref, weight_out):
+def own_kernel(payload_ref, extra_ref, own_ref, near_ref, far_ref, weight_out):
     own_ref[...] = payload_ref[...]
-    weight_out[...] = weight_ref[...]
-    near_ref[...], far_ref[...] = local_places(ids_ref[...])
+    weight_out[...] = extra_ref[OWNED:, :]
+    near_ref[...], far_ref[...] = local_places(extra_ref[0:OWNED, :].astype(jnp.int32))
 
 
 def gather_pair(table, places, first_column, blocks):
@@ -510,20 +511,20 @@
     off_lon = [(i, (i + 1 if i % 2 else i - 1) % lons) for i in range(lons)]
 
     edge = sds((EDGE_ROWS, LANES))
-    payload, first, second, near_ids, weight = pl.pallas_call(
+    payload, first, second, extra = pl.pallas_call(
         payload_kernel,
         out_shape=[
             sds((PAYLOAD, LANES)),
             edge,
             edge,
-            jax.ShapeDtypeStruct((OWNED, LANES), jnp.int32),
-            sds((OWNED, LANES)),
+            sds((2 * OWNED, LANES)),
         ],
         in_specs=[pl.BlockSpec(memory_space=pltpu.HBM)] * 8,
-        out_specs=vmem(5),
+        out_specs=vmem(4),
         scratch_shapes=[
             pltpu.VMEM((1, NOB), F32),
             pltpu.VMEM((1, NOB), jnp.int32),
+            pltpu.VMEM((OWNED, LANES), jnp.int32),
             pltpu.SemaphoreType.DMA((8,)),
         ],
         compiler_params=pltpu.CompilerParams(vmem_limit_bytes=PAYLOAD_LIMIT),
@@ -545,7 +546,7 @@
     own, near, far, weight = call(
         own_kernel,
         [sds((PAYLOAD, LANES))] + [sds((OWNED, LANES))] * 3,
-        (payload, near_ids, weight),
+        (payload, extra),
         flops=1 << 20,
     )
     send, values = call(

time: 85.5 us -> 84.8 us (level)
    unnamed x6 -> x4, local copies, waits for them, and re-layouts: 2.35 us -> 1.67 us
  transfers between devices with their start and end apart: 7 -> 7, of which waited for: 1 -> 2; matrix products, arithmetic and copies ran while one was open for 0% -> 0% of each run, Pallas kernels for 3% -> 3%
where the time goes in v6:
time: 84.8 us; the launch traced here: 84.4 us
  starting transfers between devices  43.1 us (51%)
  blocking collectives  24.1 us (28%)
  Pallas kernels  13.8 us (16%)
  local copies, waits for them, and re-layouts  1.67 us (2%)
  waiting for transfers between devices  1.51 us (2%)
    ppermute x1, starting transfers between devices, per_device(): other = lax.ppermute(payload, 'lat', [(0, 1), (1, 0)])  16.3 us
    all_to_all x1, blocking collectives, per_device(): lax.all_to_all(send.reshape(members, send.shape[2]), 'mem', split_axis=0,...  14.6 us
    pallas_call x6, Pallas kernels, call(): pl.pallas_call(kernel, out_shape=shapes, in_specs=vmem(len(operands)), ou...  12 us
    all_to_all x1, blocking collectives, per_device(): lax.all_to_all(updated, 'mem', split_axis=0, concat_axis=0, tiled=True)  9.51 us
    ppermute x1, starting transfers between devices, per_device(): second_other = lax.ppermute(second, ('lon', 'lat'), corners)  9.06 us
    ppermute x1, starting transfers between devices, per_device(): spread_second = lax.ppermute(spread, ('lon', 'lat'), off_chip)  5.19 us
    ppermute x1, starting transfers between devices, per_device(): first_other = lax.ppermute(first, ('lon', 'lat'), chip_corners)  4.77 us
    ppermute x1, starting transfers between devices, per_device(): second_in = lax.ppermute(second, 'lon', off_lon)  3.48 us
  transfers between devices with their start and end apart: 7, of which 2 were waited for; matrix products, arithmetic and copies ran while one was open for 0% of the time, Pallas kernels for 3%

profile of v6, /device:TPU:1, one launch (start us, length us, event | category | flops | bytes accessed | tf_op | source)
XLA Modules:
  0.0 84.4 jit_solution(17464444661051127377)
XLA Ops:
  0.0 1.8 %shard_map.82 = (f32[360,128]{1,0:T(8,128)}, f32[16,128]{1,0:T(8,128)}, f32[16,128]{1,0:T(8,128)}, f32[64,128]{1,0:T(8,128)}) custom-call(f32[256,128]{1,0:T(8,128)} %bitcast.16, f32[32,128]{1,0:T(8,128)} %bitcast.17, f32[32,128]{1,0:T(8,128)} %bitcast.18, f32[32,128]{1,0:T(8,128)} %bitcast.19, f32[1,256]{1,0:T(1,128)} %bitcast.20, s32[1,256]{1,0:T(1,128)} %bitcast.21, ...), custom_call_target="tpu_custom_call" | custom-call | tf_op jit(solution)/shard_map/pallas_call | solution.py:514
  1.8 16.3 %collective-permute-start = (f32[360,128]{1,0:T(8,128)}, f32[360,128]{1,0:T(8,128)S(1)}, u32[]{:S(2)}, u32[]{:S(2)}) collective-permute-start(f32[360,128]{1,0:T(8,128)} %get-tuple-element.20.payload_ref), channel_id=1, source_target_pairs={{0,1},{1,0},{2,3},{3,2},{4,5},{5,4},{6,7},{7,6},{8,9},{9,8},{10,11... | collective-permute-start | bytes 552968 | tf_op jit(solution)/shard_map/ppermute | solution.py:541
  18.1 4.8 %collective-permute-start.1 = (f32[16,128]{1,0:T(8,128)}, f32[16,128]{1,0:T(8,128)S(1)}, u32[]{:S(2)}, u32[]{:S(2)}) collective-permute-start(f32[16,128]{1,0:T(8,128)} %get-tuple-element.25), channel_id=1, source_target_pairs={{0,3},{2,1},{4,7},{6,5},{8,11},{10,9},{12,15},{14,13},{16,19},{18,... | collective-permute-start | bytes 24584 | tf_op jit(solution)/shard_map/ppermute | solution.py:542
  22.8 9.1 %collective-permute-start.2 = (f32[16,128]{1,0:T(8,128)}, f32[16,128]{1,0:T(8,128)S(1)}, u32[]{:S(2)}, u32[]{:S(2)}) collective-permute-start(f32[16,128]{1,0:T(8,128)} %get-tuple-element.26), channel_id=1, source_target_pairs={{0,31},{2,5},{4,3},{6,9},{8,7},{10,13},{12,11},{14,17},{16,15},{18... | collective-permute-start | bytes 24584 | tf_op jit(solution)/shard_map/ppermute | solution.py:543
  31.9 3.5 %collective-permute-start.3 = (f32[16,128]{1,0:T(8,128)}, f32[16,128]{1,0:T(8,128)S(1)}, u32[]{:S(2)}, u32[]{:S(2)}) collective-permute-start(f32[16,128]{1,0:T(8,128)} %get-tuple-element.26), channel_id=1, source_target_pairs={{0,30},{2,4},{4,2},{6,8},{8,6},{10,12},{12,10},{14,16},{16,14},{18... | collective-permute-start | bytes 24584 | tf_op jit(solution)/shard_map/ppermute | solution.py:544
  35.4 1.9 %collective-permute-start.4 = (f32[16,128]{1,0:T(8,128)}, f32[16,128]{1,0:T(8,128)S(1)}, u32[]{:S(2)}, u32[]{:S(2)}) collective-permute-start(f32[16,128]{1,0:T(8,128)} %get-tuple-element.25), channel_id=1, source_target_pairs={{0,2},{2,0},{4,6},{6,4},{8,10},{10,8},{12,14},{14,12},{16,18},{18,... | collective-permute-start | bytes 24584 | tf_op jit(solution)/shard_map/ppermute | solution.py:545
  37.3 0.0 copy-start
  37.3 0.9 %copy-done = f32[360,128]{1,0:T(8,128)S(1)} copy-done((f32[360,128]{1,0:T(8,128)S(1)}, f32[360,128]{1,0:T(8,128)}, u32[]{:S(2)}) %copy-start) | copy-done | bytes 184344
  38.2 0.0 copy-start.1
  38.2 0.8 copy-done.1
  39.0 0.0 collective-permute-done.1.first_other_ref
  39.0 0.3 collective-permute-done.2.second_other_ref
  39.4 0.0 collective-permute-done.3.second_ref
  39.4 0.0 collective-permute-done.4.first_ref
  39.4 0.0 collective-permute-done.other_ref
  39.4 1.9 %shard_map.84 = (f32[16,8,768]{2,1,0:T(8,128)S(1)}, f32[8,512]{1,0:T(8,128)S(1)}) custom-call(f32[360,128]{1,0:T(8,128)S(1)} %get-tuple-element.24.own_ref, f32[360,128]{1,0:T(8,128)S(1)} %collective-permute-done.other_ref, f32[16,128]{1,0:T(8,128)S(1)} %collective-permute-done.1.first_other_ref, f32[16,128]{1,0:T(8,128)S(1)} %collective-permute-done.2.second_other_ref, ...), custom_call_target="tpu_custom_call" | custom-call | tf_op jit(solution)/shard_map/pallas_call | solution.py:479
  41.3 14.6 %all_to_all.17 = f32[16,8,768]{2,1,0:T(8,128)S(1)} all-to-all(f32[16,8,768]{2,1,0:T(8,128)S(1)} %get-tuple-element.27), channel_id=1, replica_groups=mesh['mem'=16,'lon'=16,'lat'=2] {'mem'}, dimensions={0} | all-to-all | bytes 786432 | tf_op jit(solution)/shard_map/all_to_all | solution.py:559
  55.9 0.1 shard_map.85
  56.0 5.2 %collective-permute-start.5 = (f32[136,512]{1,0:T(8,128)S(1)}, f32[136,512]{1,0:T(8,128)S(1)}, u32[]{:S(2)}, u32[]{:S(2)}) collective-permute-start(f32[136,512]{1,0:T(8,128)S(1)} %get-tuple-element.29.mine_ref), channel_id=1, source_target_pairs={{0,31},{2,4},{4,2},{6,8},{8,6},{10,12},{12,10},{14,16},{16,14},{18... | collective-permute-start | bytes 835592 | tf_op jit(solution)/shard_map/ppermute | solution.py:567
  61.2 2.4 %collective-permute-start.6 = (f32[129,512]{1,0:T(8,128)S(1)}, f32[129,512]{1,0:T(8,128)S(1)}, u32[]{:S(2)}, u32[]{:S(2)}) collective-permute-start(f32[129,512]{1,0:T(8,128)S(1)} %get-tuple-element.31), channel_id=1, source_target_pairs={{0,2},{2,0},{4,6},{6,4},{8,10},{10,8},{12,14},{14,12},{16,18},{18,... | collective-permute-start | bytes 792584 | tf_op jit(solution)/shard_map/ppermute | solution.py:568
  63.6 1.2 %collective-permute-done.6.first_ref = f32[129,512]{1,0:T(8,128)S(1)} collective-permute-done((f32[129,512]{1,0:T(8,128)S(1)}, f32[129,512]{1,0:T(8,128)S(1)}, u32[]{:S(2)}, u32[]{:S(2)}) %collective-permute-start.6) | collective-permute-done | bytes 264224 | tf_op jit(solution)/shard_map/ppermute | solution.py:568
  64.8 2.5 %shard_map.86 = (f32[32,136,128]{2,1,0:T(8,128)S(1)}, f32[256,128]{1,0:T(8,128)S(1)}, f32[256,128]{1,0:T(8,128)S(1)}) custom-call(f32[128,768]{1,0:T(8,128)S(1)} %bitcast.12, f32[32,128]{1,0:T(8,128)S(1)} %get-tuple-element.30.places, f32[136,512]{1,0:T(8,128)S(1)} %get-tuple-element.29.mine_ref, f32[129,512]{1,0:T(8,128)S(1)} %collective-permute-done.6.first_ref), custom_call_target="tpu_custom_call" | custom-call | tf_op jit(solution)/shard_map/pallas_call | solution.py:479
  67.3 0.0 collective-permute-done.5.second_ref
  67.3 6.8 %shard_map.87 = f32[128,256]{1,0:T(8,128)S(1)} custom-call(f32[32,128]{1,0:T(8,128)S(1)} %get-tuple-element.22.places, f32[32,128]{1,0:T(8,128)S(1)} %get-tuple-element.23.weight_ref, f32[136,512]{1,0:T(8,128)S(1)} %collective-permute-done.5.second_ref, f32[32,136,128]{2,1,0:T(8,128)S(1)} %get-tuple-element.32.part_ref, ...), custom_call_target="tpu_custom_call" | custom-call | flops 3758096384 | bytes 4194304 | tf_op jit(solution)/shard_map/pallas_call | solution.py:479
  74.0 9.5 %all_to_all.18.recv_ref = f32[16,8,256]{2,1,0:T(8,128)S(1)} all-to-all(f32[16,8,256]{2,1,0:T(8,128)S(1)} %bitcast.13), channel_id=1, replica_groups=mesh['mem'=16,'lon'=16,'lat'=2] {'mem'}, dimensions={0} | all-to-all | bytes 262144 | tf_op jit(solution)/shard_map/all_to_all | solution.py:590
  83.6 0.8 shard_map.88
  (1 shorter events, 0.0 us)
Async XLA Ops:
  1.8 37.6 %collective-permute-start = (f32[360,128]{1,0:T(8,128)}, f32[360,128]{1,0:T(8,128)S(1)}, u32[]{:S(2)}, u32[]{:S(2)}) collective-permute-start(f32[360,128]{1,0:T(8,128)} %get-tuple-element.20.payload_ref), channel_id=1, source_target_pairs={{0,1},{1,0},{2,3},{3,2},{4,5},{5,4},{6,7},{7,6},{8,9},{9,8},{10,11... | collective-permute-start | bytes 552968 | tf_op jit(solution)/shard_map/ppermute | solution.py:541
  18.1 21.0 %collective-permute-start.1 = (f32[16,128]{1,0:T(8,128)}, f32[16,128]{1,0:T(8,128)S(1)}, u32[]{:S(2)}, u32[]{:S(2)}) collective-permute-start(f32[16,128]{1,0:T(8,128)} %get-tuple-element.25), channel_id=1, source_target_pairs={{0,3},{2,1},{4,7},{6,5},{8,11},{10,9},{12,15},{14,13},{16,19},{18,... | collective-permute-start | bytes 24584 | tf_op jit(solution)/shard_map/ppermute | solution.py:542
  22.8 16.5 %collective-permute-start.2 = (f32[16,128]{1,0:T(8,128)}, f32[16,128]{1,0:T(8,128)S(1)}, u32[]{:S(2)}, u32[]{:S(2)}) collective-permute-start(f32[16,128]{1,0:T(8,128)} %get-tuple-element.26), channel_id=1, source_target_pairs={{0,31},{2,5},{4,3},{6,9},{8,7},{10,13},{12,11},{14,17},{16,15},{18... | collective-permute-start | bytes 24584 | tf_op jit(solution)/shard_map/ppermute | solution.py:543
  31.9 7.5 %collective-permute-start.3 = (f32[16,128]{1,0:T(8,128)}, f32[16,128]{1,0:T(8,128)S(1)}, u32[]{:S(2)}, u32[]{:S(2)}) collective-permute-start(f32[16,128]{1,0:T(8,128)} %get-tuple-element.26), channel_id=1, source_target_pairs={{0,30},{2,4},{4,2},{6,8},{8,6},{10,12},{12,10},{14,16},{16,14},{18... | collective-permute-start | bytes 24584 | tf_op jit(solution)/shard_map/ppermute | solution.py:544
  35.4 4.0 %collective-permute-start.4 = (f32[16,128]{1,0:T(8,128)}, f32[16,128]{1,0:T(8,128)S(1)}, u32[]{:S(2)}, u32[]{:S(2)}) collective-permute-start(f32[16,128]{1,0:T(8,128)} %get-tuple-element.25), channel_id=1, source_target_pairs={{0,2},{2,0},{4,6},{6,4},{8,10},{10,8},{12,14},{14,12},{16,18},{18,... | collective-permute-start | bytes 24584 | tf_op jit(solution)/shard_map/ppermute | solution.py:545
  37.3 0.9 %copy-start = (f32[360,128]{1,0:T(8,128)S(1)}, f32[360,128]{1,0:T(8,128)}, u32[]{:S(2)}) copy-start(f32[360,128]{1,0:T(8,128)} %get-tuple-element.20.payload_ref) | copy-start | bytes 552964
  38.2 0.8 copy-start.1
  56.0 11.3 %collective-permute-start.5 = (f32[136,512]{1,0:T(8,128)S(1)}, f32[136,512]{1,0:T(8,128)S(1)}, u32[]{:S(2)}, u32[]{:S(2)}) collective-permute-start(f32[136,512]{1,0:T(8,128)S(1)} %get-tuple-element.29.mine_ref), channel_id=1, source_target_pairs={{0,31},{2,4},{4,2},{6,8},{8,6},{10,12},{12,10},{14,16},{16,14},{18... | collective-permute-start | bytes 835592 | tf_op jit(solution)/shard_map/ppermute | solution.py:567
  61.2 3.6 %collective-permute-start.6 = (f32[129,512]{1,0:T(8,128)S(1)}, f32[129,512]{1,0:T(8,128)S(1)}, u32[]{:S(2)}, u32[]{:S(2)}) collective-permute-start(f32[129,512]{1,0:T(8,128)S(1)} %get-tuple-element.31), channel_id=1, source_target_pairs={{0,2},{2,0},{4,6},{6,4},{8,10},{10,8},{12,14},{14,12},{16,18},{18,... | collective-permute-start | bytes 792584 | tf_op jit(solution)/shard_map/ppermute | solution.py:568

commit v7 on v6

--- a/solution.py
+++ b/solution.py
@@ -107,14 +107,8 @@
     copies = [pltpu.make_async_copy(src, dst, sems.at[n]) for n, (src, dst) in enumerate(moves)]
     for copy in copies:
         copy.start()
-    for copy in copies:
+    for copy in copies[:4]:
         copy.wait()
-    extra_ref[0:OWNED, :] = ids[...].astype(F32)
-    values = value[...]
-    sites = site[...].astype(F32)
-    rest = jnp.zeros((PAYLOAD - SITE_ROW - 2, LANES), F32)
-    pieces = [values[:, :LANES], values[:, LANES:], sites[:, :LANES], sites[:, LANES:], rest]
-    out_ref[VALUE_ROW:, :] = jnp.concatenate(pieces, axis=0)
     lane = lane_index()
     even = scalar_mask(lon_parity(), 0)
     for tile in range(2):
@@ -130,6 +124,14 @@
             right = jnp.where(place, roll(x, 4 * slot + 4), right)
         first_ref[tile * 8 : tile * 8 + 8, :] = jnp.where(even, right, left)
         second_ref[tile * 8 : tile * 8 + 8, :] = jnp.where(even, left, right)
+    for copy in copies[4:]:
+        copy.wait()
+    extra_ref[0:OWNED, :] = ids[...].astype(F32)
+    values = value[...]
+    sites = site[...].astype(F32)
+    rest = jnp.zeros((PAYLOAD - SITE_ROW - 2, LANES), F32)
+    pieces = [values[:, :LANES], values[:, LANES:], sites[:, :LANES], sites[:, LANES:], rest]
+    out_ref[VALUE_ROW:, :] = jnp.concatenate(pieces, axis=0)
 
 
 def advance_in_time(q, coef, level, first_lane, last_lane):

time: 84.8 us -> 84.9 us (level)
  no operation moved by 1% of the time
where the time goes in v7:
time: 84.9 us; the launch traced here: 84.5 us
  starting transfers between devices  43.1 us (51%)
  blocking collectives  24.1 us (28%)
  Pallas kernels  13.9 us (16%)
  local copies, waits for them, and re-layouts  1.67 us (2%)
  waiting for transfers between devices  1.51 us (2%)
    ppermute x1, starting transfers between devices, per_device(): other = lax.ppermute(payload, 'lat', [(0, 1), (1, 0)])  16.3 us
    all_to_all x1, blocking collectives, per_device(): lax.all_to_all(send.reshape(members, send.shape[2]), 'mem', split_axis=0,...  14.6 us
    pallas_call x6, Pallas kernels, call(): pl.pallas_call(kernel, out_shape=shapes, in_specs=vmem(len(operands)), ou...  12 us
    all_to_all x1, blocking collectives, per_device(): lax.all_to_all(updated, 'mem', split_axis=0, concat_axis=0, tiled=True)  9.51 us
    ppermute x1, starting transfers between devices, per_device(): second_other = lax.ppermute(second, ('lon', 'lat'), corners)  9.06 us
    ppermute x1, starting transfers between devices, per_device(): spread_second = lax.ppermute(spread, ('lon', 'lat'), off_chip)  5.2 us
    ppermute x1, starting transfers between devices, per_device(): first_other = lax.ppermute(first, ('lon', 'lat'), chip_corners)  4.77 us
    ppermute x1, starting transfers between devices, per_device(): second_in = lax.ppermute(second, 'lon', off_lon)  3.48 us
  transfers between devices with their start and end apart: 7, of which 2 were waited for; matrix products, arithmetic and copies ran while one was open for 0% of the time, Pallas kernels for 3%

profile of v7, /device:TPU:1, one launch (start us, length us, event | category | flops | bytes accessed | tf_op | source)
XLA Modules:
  0.0 84.5 jit_solution(6255174768651401072)
XLA Ops:
  0.0 1.8 %shard_map.82 = (f32[360,128]{1,0:T(8,128)}, f32[16,128]{1,0:T(8,128)}, f32[16,128]{1,0:T(8,128)}, f32[64,128]{1,0:T(8,128)}) custom-call(f32[256,128]{1,0:T(8,128)} %bitcast.16, f32[32,128]{1,0:T(8,128)} %bitcast.17, f32[32,128]{1,0:T(8,128)} %bitcast.18, f32[32,128]{1,0:T(8,128)} %bitcast.19, f32[1,256]{1,0:T(1,128)} %bitcast.20, s32[1,256]{1,0:T(1,128)} %bitcast.21, ...), custom_call_target="tpu_custom_call" | custom-call | tf_op jit(solution)/shard_map/pallas_call | solution.py:516
  1.9 16.3 %collective-permute-start = (f32[360,128]{1,0:T(8,128)}, f32[360,128]{1,0:T(8,128)S(1)}, u32[]{:S(2)}, u32[]{:S(2)}) collective-permute-start(f32[360,128]{1,0:T(8,128)} %get-tuple-element.20.payload_ref), channel_id=1, source_target_pairs={{0,1},{1,0},{2,3},{3,2},{4,5},{5,4},{6,7},{7,6},{8,9},{9,8},{10,11... | collective-permute-start | bytes 552968 | tf_op jit(solution)/shard_map/ppermute | solution.py:543
  18.1 4.8 %collective-permute-start.1 = (f32[16,128]{1,0:T(8,128)}, f32[16,128]{1,0:T(8,128)S(1)}, u32[]{:S(2)}, u32[]{:S(2)}) collective-permute-start(f32[16,128]{1,0:T(8,128)} %get-tuple-element.25), channel_id=1, source_target_pairs={{0,3},{2,1},{4,7},{6,5},{8,11},{10,9},{12,15},{14,13},{16,19},{18,... | collective-permute-start | bytes 24584 | tf_op jit(solution)/shard_map/ppermute | solution.py:544
  22.9 9.1 %collective-permute-start.2 = (f32[16,128]{1,0:T(8,128)}, f32[16,128]{1,0:T(8,128)S(1)}, u32[]{:S(2)}, u32[]{:S(2)}) collective-permute-start(f32[16,128]{1,0:T(8,128)} %get-tuple-element.26), channel_id=1, source_target_pairs={{0,31},{2,5},{4,3},{6,9},{8,7},{10,13},{12,11},{14,17},{16,15},{18... | collective-permute-start | bytes 24584 | tf_op jit(solution)/shard_map/ppermute | solution.py:545
  32.0 3.5 %collective-permute-start.3 = (f32[16,128]{1,0:T(8,128)}, f32[16,128]{1,0:T(8,128)S(1)}, u32[]{:S(2)}, u32[]{:S(2)}) collective-permute-start(f32[16,128]{1,0:T(8,128)} %get-tuple-element.26), channel_id=1, source_target_pairs={{0,30},{2,4},{4,2},{6,8},{8,6},{10,12},{12,10},{14,16},{16,14},{18... | collective-permute-start | bytes 24584 | tf_op jit(solution)/shard_map/ppermute | solution.py:546
  35.5 1.9 %collective-permute-start.4 = (f32[16,128]{1,0:T(8,128)}, f32[16,128]{1,0:T(8,128)S(1)}, u32[]{:S(2)}, u32[]{:S(2)}) collective-permute-start(f32[16,128]{1,0:T(8,128)} %get-tuple-element.25), channel_id=1, source_target_pairs={{0,2},{2,0},{4,6},{6,4},{8,10},{10,8},{12,14},{14,12},{16,18},{18,... | collective-permute-start | bytes 24584 | tf_op jit(solution)/shard_map/ppermute | solution.py:547
  37.4 0.0 copy-start
  37.4 0.9 %copy-done = f32[360,128]{1,0:T(8,128)S(1)} copy-done((f32[360,128]{1,0:T(8,128)S(1)}, f32[360,128]{1,0:T(8,128)}, u32[]{:S(2)}) %copy-start) | copy-done | bytes 184344
  38.3 0.0 copy-start.1
  38.3 0.8 copy-done.1
  39.1 0.0 collective-permute-done.1.first_other_ref
  39.1 0.3 collective-permute-done.2.second_other_ref
  39.4 0.0 collective-permute-done.3.second_ref
  39.5 0.0 collective-permute-done.4.first_ref
  39.5 0.0 collective-permute-done.other_ref
  39.5 1.9 %shard_map.84 = (f32[16,8,768]{2,1,0:T(8,128)S(1)}, f32[8,512]{1,0:T(8,128)S(1)}) custom-call(f32[360,128]{1,0:T(8,128)S(1)} %get-tuple-element.24.own_ref, f32[360,128]{1,0:T(8,128)S(1)} %collective-permute-done.other_ref, f32[16,128]{1,0:T(8,128)S(1)} %collective-permute-done.1.first_other_ref, f32[16,128]{1,0:T(8,128)S(1)} %collective-permute-done.2.second_other_ref, ...), custom_call_target="tpu_custom_call" | custom-call | tf_op jit(solution)/shard_map/pallas_call | solution.py:481
  41.3 14.6 %all_to_all.17 = f32[16,8,768]{2,1,0:T(8,128)S(1)} all-to-all(f32[16,8,768]{2,1,0:T(8,128)S(1)} %get-tuple-element.27), channel_id=1, replica_groups=mesh['mem'=16,'lon'=16,'lat'=2] {'mem'}, dimensions={0} | all-to-all | bytes 786432 | tf_op jit(solution)/shard_map/all_to_all | solution.py:561
  56.0 0.1 shard_map.85
  56.1 5.2 %collective-permute-start.5 = (f32[136,512]{1,0:T(8,128)S(1)}, f32[136,512]{1,0:T(8,128)S(1)}, u32[]{:S(2)}, u32[]{:S(2)}) collective-permute-start(f32[136,512]{1,0:T(8,128)S(1)} %get-tuple-element.29.mine_ref), channel_id=1, source_target_pairs={{0,31},{2,4},{4,2},{6,8},{8,6},{10,12},{12,10},{14,16},{16,14},{18... | collective-permute-start | bytes 835592 | tf_op jit(solution)/shard_map/ppermute | solution.py:569
  61.3 2.4 %collective-permute-start.6 = (f32[129,512]{1,0:T(8,128)S(1)}, f32[129,512]{1,0:T(8,128)S(1)}, u32[]{:S(2)}, u32[]{:S(2)}) collective-permute-start(f32[129,512]{1,0:T(8,128)S(1)} %get-tuple-element.31), channel_id=1, source_target_pairs={{0,2},{2,0},{4,6},{6,4},{8,10},{10,8},{12,14},{14,12},{16,18},{18,... | collective-permute-start | bytes 792584 | tf_op jit(solution)/shard_map/ppermute | solution.py:570
  63.7 1.2 %collective-permute-done.6.first_ref = f32[129,512]{1,0:T(8,128)S(1)} collective-permute-done((f32[129,512]{1,0:T(8,128)S(1)}, f32[129,512]{1,0:T(8,128)S(1)}, u32[]{:S(2)}, u32[]{:S(2)}) %collective-permute-start.6) | collective-permute-done | bytes 264224 | tf_op jit(solution)/shard_map/ppermute | solution.py:570
  64.9 2.5 %shard_map.86 = (f32[32,136,128]{2,1,0:T(8,128)S(1)}, f32[256,128]{1,0:T(8,128)S(1)}, f32[256,128]{1,0:T(8,128)S(1)}) custom-call(f32[128,768]{1,0:T(8,128)S(1)} %bitcast.12, f32[32,128]{1,0:T(8,128)S(1)} %get-tuple-element.30.places, f32[136,512]{1,0:T(8,128)S(1)} %get-tuple-element.29.mine_ref, f32[129,512]{1,0:T(8,128)S(1)} %collective-permute-done.6.first_ref), custom_call_target="tpu_custom_call" | custom-call | tf_op jit(solution)/shard_map/pallas_call | solution.py:481
  67.3 0.0 collective-permute-done.5.second_ref
  67.4 6.8 %shard_map.87 = f32[128,256]{1,0:T(8,128)S(1)} custom-call(f32[32,128]{1,0:T(8,128)S(1)} %get-tuple-element.22.places, f32[32,128]{1,0:T(8,128)S(1)} %get-tuple-element.23.weight_ref, f32[136,512]{1,0:T(8,128)S(1)} %collective-permute-done.5.second_ref, f32[32,136,128]{2,1,0:T(8,128)S(1)} %get-tuple-element.32.part_ref, ...), custom_call_target="tpu_custom_call" | custom-call | flops 3758096384 | bytes 4194304 | tf_op jit(solution)/shard_map/pallas_call | solution.py:481
  74.1 9.5 %all_to_all.18.recv_ref = f32[16,8,256]{2,1,0:T(8,128)S(1)} all-to-all(f32[16,8,256]{2,1,0:T(8,128)S(1)} %bitcast.13), channel_id=1, replica_groups=mesh['mem'=16,'lon'=16,'lat'=2] {'mem'}, dimensions={0} | all-to-all | bytes 262144 | tf_op jit(solution)/shard_map/all_to_all | solution.py:592
  83.6 0.8 shard_map.88
  (1 shorter events, 0.0 us)
Async XLA Ops:
  1.9 37.6 %collective-permute-start = (f32[360,128]{1,0:T(8,128)}, f32[360,128]{1,0:T(8,128)S(1)}, u32[]{:S(2)}, u32[]{:S(2)}) collective-permute-start(f32[360,128]{1,0:T(8,128)} %get-tuple-element.20.payload_ref), channel_id=1, source_target_pairs={{0,1},{1,0},{2,3},{3,2},{4,5},{5,4},{6,7},{7,6},{8,9},{9,8},{10,11... | collective-permute-start | bytes 552968 | tf_op jit(solution)/shard_map/ppermute | solution.py:543
  18.1 21.0 %collective-permute-start.1 = (f32[16,128]{1,0:T(8,128)}, f32[16,128]{1,0:T(8,128)S(1)}, u32[]{:S(2)}, u32[]{:S(2)}) collective-permute-start(f32[16,128]{1,0:T(8,128)} %get-tuple-element.25), channel_id=1, source_target_pairs={{0,3},{2,1},{4,7},{6,5},{8,11},{10,9},{12,15},{14,13},{16,19},{18,... | collective-permute-start | bytes 24584 | tf_op jit(solution)/shard_map/ppermute | solution.py:544
  22.9 16.5 %collective-permute-start.2 = (f32[16,128]{1,0:T(8,128)}, f32[16,128]{1,0:T(8,128)S(1)}, u32[]{:S(2)}, u32[]{:S(2)}) collective-permute-start(f32[16,128]{1,0:T(8,128)} %get-tuple-element.26), channel_id=1, source_target_pairs={{0,31},{2,5},{4,3},{6,9},{8,7},{10,13},{12,11},{14,17},{16,15},{18... | collective-permute-start | bytes 24584 | tf_op jit(solution)/shard_map/ppermute | solution.py:545
  32.0 7.5 %collective-permute-start.3 = (f32[16,128]{1,0:T(8,128)}, f32[16,128]{1,0:T(8,128)S(1)}, u32[]{:S(2)}, u32[]{:S(2)}) collective-permute-start(f32[16,128]{1,0:T(8,128)} %get-tuple-element.26), channel_id=1, source_target_pairs={{0,30},{2,4},{4,2},{6,8},{8,6},{10,12},{12,10},{14,16},{16,14},{18... | collective-permute-start | bytes 24584 | tf_op jit(solution)/shard_map/ppermute | solution.py:546
  35.5 4.0 %collective-permute-start.4 = (f32[16,128]{1,0:T(8,128)}, f32[16,128]{1,0:T(8,128)S(1)}, u32[]{:S(2)}, u32[]{:S(2)}) collective-permute-start(f32[16,128]{1,0:T(8,128)} %get-tuple-element.25), channel_id=1, source_target_pairs={{0,2},{2,0},{4,6},{6,4},{8,10},{10,8},{12,14},{14,12},{16,18},{18,... | collective-permute-start | bytes 24584 | tf_op jit(solution)/shard_map/ppermute | solution.py:547
  37.4 0.9 %copy-start = (f32[360,128]{1,0:T(8,128)S(1)}, f32[360,128]{1,0:T(8,128)}, u32[]{:S(2)}) copy-start(f32[360,128]{1,0:T(8,128)} %get-tuple-element.20.payload_ref) | copy-start | bytes 552964
  38.3 0.8 copy-start.1
  56.1 11.3 %collective-permute-start.5 = (f32[136,512]{1,0:T(8,128)S(1)}, f32[136,512]{1,0:T(8,128)S(1)}, u32[]{:S(2)}, u32[]{:S(2)}) collective-permute-start(f32[136,512]{1,0:T(8,128)S(1)} %get-tuple-element.29.mine_ref), channel_id=1, source_target_pairs={{0,31},{2,4},{4,2},{6,8},{8,6},{10,12},{12,10},{14,16},{16,14},{18... | collective-permute-start | bytes 835592 | tf_op jit(solution)/shard_map/ppermute | solution.py:569
  61.3 3.6 %collective-permute-start.6 = (f32[129,512]{1,0:T(8,128)S(1)}, f32[129,512]{1,0:T(8,128)S(1)}, u32[]{:S(2)}, u32[]{:S(2)}) collective-permute-start(f32[129,512]{1,0:T(8,128)S(1)} %get-tuple-element.31), channel_id=1, source_target_pairs={{0,2},{2,0},{4,6},{6,4},{8,10},{10,8},{12,14},{14,12},{16,18},{18,... | collective-permute-start | bytes 792584 | tf_op jit(solution)/shard_map/ppermute | solution.py:570
